TPU v7x, 128 devices: a whole 4x4x4 slice. The times are simulated.
128 devices in a mesh: seq: 16 (over z, x), head: 8 (over y, core).
Axes of the slice: x: 4, y: 4, z: 4, core: 2. Of those that a mesh axis runs over, the one named last changes fastest.
Arguments:
- hidden: bfloat16 [2, 4, 8192], P(None, None, 'seq'), may hold values from -6 to 6
- w_query: bfloat16 [8192, 8192], P('seq', 'head'), may hold values from -0.0625 to 0.0625
- key_matrix: bfloat16 [8192, 1024], P('seq', 'head'), may hold values from -0.25 to 0.25
- value_matrix: bfloat16 [8192, 1024], P('seq', 'head'), may hold values from -0.0625 to 0.0625
- w_out: bfloat16 [8192, 8192], P('head', 'seq'), may hold values from -0.0625 to 0.0625
- key_cache: bfloat16 [4, 131072, 1024], P(None, 'seq', 'head'), may hold values from -250 to 250, as said below
- stored_value_cache: bfloat16 [4, 131072, 1024], P(None, 'seq', 'head'), may hold values from -6 to 6
- lengths: int32 [4], replicated, may hold values from 8192 to 131072, as said below
Outputs:
- attn_out: bfloat16 [2, 4, 8192], P(None, None, ('seq', 'head'))
- new_keys: bfloat16 [2, 4, 1024], P(None, None, 'head')
- new_values: bfloat16 [2, 4, 1024], P(None, None, 'head')
Inputs may be any that keep to these rules, and one draw needn't show every extreme that they name: `key_cache`: cached keys, already rotated to their positions. `lengths`: in every draw one sequence fills all 131072 cached positions.
All inputs are finite; a program needn't handle non-finite values.
Results may differ from a plain program's by a relative error of at most 0.02.
Values may be sent and summed in bfloat16 or wider, within the bound.
No kernel may reach another device: no remote copies, remote signals or barrier semaphores. Data moves between devices by JAX's collectives and lax.ppermute only.
A program may use at most 64 MiB of HBM per device.

v0:
```python
import jax
import jax.numpy as jnp
import numpy as np
from jax import lax
from jax.sharding import PartitionSpec as P

HEAD_WIDTH = 128
BLOCK_POSITIONS = 512


theta_base = 500000.0
negative_fill = -1e30


def apply_rotary(input_vectors, token_positions):
    half_dim = input_vectors.shape[-1] // 2
    exponent = np.arange(half_dim) * 2.0 / input_vectors.shape[-1]
    inverse = theta_base ** (-exponent)
    coarse = np.mod(1024.0 * inverse, 2.0 * np.pi)
    fine_table = jnp.asarray(inverse, jnp.float32)
    coarse_table = jnp.asarray(coarse, jnp.float32)
    upper_part = (token_positions // 1024).astype(jnp.float32)[..., None]
    lower_part = (token_positions % 1024).astype(jnp.float32)[..., None]
    angles = upper_part * coarse_table + lower_part * fine_table
    cosine = jnp.cos(angles)
    sine_part = jnp.sin(angles)
    first_half = input_vectors[..., :half_dim]
    second_half = input_vectors[..., half_dim:]
    return jnp.concatenate(
        [
            first_half * cosine - second_half * sine_part,
            second_half * cosine + first_half * sine_part,
        ],
        axis=-1,
    )


def local(hidden, w_query, key_matrix, value_matrix, w_out, key_cache, stored_value_cache, lengths):
    step_count = hidden.shape[0]
    batch_size = hidden.shape[1]
    kv_local = key_matrix.shape[1] // HEAD_WIDTH
    q_local = w_query.shape[1] // HEAD_WIDTH
    queries_per_group = q_local // kv_local
    ctx_local = key_cache.shape[1]
    softmax_blocks = ctx_local // BLOCK_POSITIONS
    seq_index = lax.axis_index("seq")
    score_scale = HEAD_WIDTH ** (-0.5)
    cached_keys = key_cache.reshape(
        batch_size, softmax_blocks, BLOCK_POSITIONS, kv_local, HEAD_WIDTH
    )
    cached_values = stored_value_cache.reshape(
        batch_size, softmax_blocks, BLOCK_POSITIONS, kv_local, HEAD_WIDTH
    )
    offsets = seq_index * ctx_local + jnp.arange(ctx_local, dtype=jnp.int32).reshape(
        softmax_blocks, BLOCK_POSITIONS
    )
    valid = (offsets[None] < lengths[:, None, None])[:, None, None]

    def projections(step_inputs):
        return (
            jnp.dot(step_inputs, w_query, preferred_element_type=jnp.float32),
            jnp.dot(step_inputs, key_matrix, preferred_element_type=jnp.float32),
            jnp.dot(step_inputs, value_matrix, preferred_element_type=jnp.float32),
        )

    step_parts = [
        lax.psum(projections(hidden[step_index]), "seq") for step_index in range(step_count)
    ]
    newest_keys = []
    newest_values = []
    raw_values = []
    head_rows = []
    for step_index in range(step_count):
        query_sum, key_sum, value_sum = step_parts[step_index]
        token_positions = (lengths + step_index)[:, None]
        query_rows = (
            apply_rotary(query_sum.reshape(batch_size, q_local, HEAD_WIDTH), token_positions)
            * score_scale
        ).astype(jnp.bfloat16)
        query_rows = query_rows.reshape(batch_size, kv_local, queries_per_group, HEAD_WIDTH)
        appended_key = apply_rotary(
            key_sum.reshape(batch_size, kv_local, HEAD_WIDTH), token_positions
        ).astype(jnp.bfloat16)
        newest_keys.append(appended_key.reshape(batch_size, 1, kv_local * HEAD_WIDTH))
        newest_values.append(
            value_sum.astype(jnp.bfloat16).reshape(batch_size, 1, kv_local * HEAD_WIDTH)
        )
        raw_values.append(value_sum.reshape(batch_size, 1, kv_local * HEAD_WIDTH))
        scores = jnp.einsum(
            "bkgd,bntkd->bkgnt", query_rows, cached_keys, preferred_element_type=jnp.float32
        )
        block_top = jnp.max(jnp.where(valid, scores, negative_fill), axis=-1)
        weights = jnp.where(valid, jnp.exp(scores - block_top[..., None]), 0.0).astype(jnp.bfloat16)
        block_sum = jnp.sum(weights.astype(jnp.float32), axis=-1)
        block_out = jnp.einsum(
            "bkgnt,bntkd->bkgnd", weights, cached_values, preferred_element_type=jnp.float32
        )
        known_keys = jnp.concatenate(newest_keys, axis=1)
        known_values = jnp.concatenate(raw_values, axis=1)
        newest_count = known_keys.shape[1]
        fresh_scores = jnp.einsum(
            "bkgd,btkd->bkgt",
            query_rows,
            known_keys.reshape(batch_size, newest_count, kv_local, HEAD_WIDTH),
            preferred_element_type=jnp.float32,
        )
        fresh_top = jnp.max(fresh_scores, axis=-1)
        fresh_weights = (
            jnp.exp(fresh_scores - fresh_top[..., None]).astype(jnp.bfloat16).astype(jnp.float32)
        )
        fresh_sum = jnp.sum(fresh_weights, axis=-1)
        fresh_out = jnp.einsum(
            "bkgt,btkd->bkgd",
            fresh_weights,
            known_values.reshape(batch_size, newest_count, kv_local, HEAD_WIDTH),
        )
        local_top = jnp.max(block_top, axis=-1)
        global_top = lax.pmax(local_top, "seq")
        overall = jnp.maximum(global_top, fresh_top)
        factors = jnp.exp(block_top - overall[..., None])
        part_sum = jnp.sum(factors * block_sum, axis=-1)
        part_out = jnp.sum(factors[..., None] * block_out, axis=3)
        summed, mixed = lax.psum((part_sum, part_out), "seq")
        fresh_factor = jnp.exp(fresh_top - overall)
        summed = summed + fresh_factor * fresh_sum
        mixed = mixed + fresh_factor[..., None] * fresh_out
        head_rows.append(
            (mixed / summed[..., None])
            .astype(jnp.bfloat16)
            .reshape(batch_size, q_local * HEAD_WIDTH)
        )
    attended = jnp.stack(head_rows).reshape(step_count * batch_size, q_local * HEAD_WIDTH)
    kept_rows = w_out.shape[1] // lax.axis_size("head")
    projected = lax.psum_scatter(
        lax.dot_general(
            w_out, attended, (((0,), (1,)), ((), ())), preferred_element_type=jnp.float32
        ).astype(jnp.bfloat16),
        "head",
        scatter_dimension=0,
        tiled=True,
    ).astype(jnp.float32)
    attn_out = projected.T.reshape(step_count, batch_size, kept_rows).astype(jnp.bfloat16)
    new_keys = jnp.transpose(jnp.concatenate(newest_keys, axis=1), (1, 0, 2))
    new_values = jnp.transpose(jnp.concatenate(newest_values, axis=1), (1, 0, 2))
    return (attn_out, new_keys, new_values)


def solution(mesh):
    in_specs = (
        P(None, None, "seq"),
        P("seq", "head"),
        P("seq", "head"),
        P("seq", "head"),
        P("head", "seq"),
        P(None, "seq", "head"),
        P(None, "seq", "head"),
        P(),
    )
    out_specs = (P(None, None, ("seq", "head")), P(None, None, "head"), P(None, None, "head"))
    return jax.shard_map(local, mesh=mesh, in_specs=in_specs, out_specs=out_specs, check_vma=False)
```

profile of v0, /device:TPU:1, one launch (start us, length us, event | category | flops | bytes accessed | tf_op | source)
XLA Modules:
  0.0 254.1 jit_solution(13973917319229672429)
XLA Ops:
  7.2 0.0 copy-start
  7.2 0.0 copy-start.3
  7.2 0.0 copy-start.4
  7.2 0.0 reduce-scatter.4.cloned.1.call-start
  7.3 1.1 copy-done
  8.4 0.9 convolution_bitcast_fusion.2
  9.3 0.9 convolution_bitcast_fusion.3
  10.3 1.1 convolution_bitcast_fusion.4
  11.3 1.1 convolution_bitcast_fusion.5
  12.4 1.1 fusion.17
  13.4 1.1 fusion.21
  14.5 0.7 fusion.54
  15.2 0.7 broadcast_compare_fusion
  16.0 62.3 %all-reduce.1 = (f32[4,8,128]{2,1,0:T(8,128)S(1)}, f32[4,8,128]{2,1,0:T(8,128)S(1)}, f32[4,1,128]{2,0,1:T(4,128)S(1)}, f32[4,1,128]{2,0,1:T(4,128)S(1)}) all-reduce(f32[4,8,128]{2,1,0:T(8,128)S(1)} %bitcast.172, f32[4,8,128]{2,1,0:T(8,128)S(1)} %bitcast.171, ...), channel_id=1, replica_groups=mesh['seq'=16,'head'=8] {'seq'}, use_global_device_ids=true, to_apply=%region_0.0 | all-reduce | flops 9216 | bytes 73728 | tf_op jit(solution)/shard_map/psum | solution.py:67
  78.2 0.0 copy-start.1
  78.2 0.9 fusion.42
  79.2 0.1 multiply_subtract_fusion
  79.3 0.1 fusion.10
  79.3 5.9 %fusion.13 = f32[4,8,16,512]{3,1,2,0:T(8,128)S(1)} fusion(bf16[4,16,512,128]{3,2,1,0:T(8,128)(2,1)} %bitcast.167, bf16[4,8,128]{2,1,0:T(8,128)(2,1)S(1)} %fusion.10), kind=kOutput, calls=%fused_computation.45 | convolution fusion | flops 67108864 | bytes 9445376 | tf_op jit(solution)/shard_map/bkgd,bntkd->bkgnt/dot_general | solution.py:89
  85.2 0.0 copy-done.3
  85.2 0.0 copy-done.4
  85.2 0.1 subtract_convert_fusion.1
  85.4 0.1 maximum_maximum_fusion
  85.4 0.1 fusion.59
  85.6 0.1 fusion.9
  85.7 0.1 maximum_bitcast_fusion.2
  85.7 0.1 fusion.47
  85.9 0.0 copy-done.1
  85.9 2.4 select_reduce_fusion.3
  88.3 1.0 convert_reduce_fusion.1
  89.3 28.5 %all-reduce.2 = (f32[4,1,8]{2,0,1:T(4,128)S(1)}, f32[4,1,8]{2,0,1:T(4,128)S(1)}) all-reduce(f32[4,1,8]{2,0,1:T(4,128)S(1)} %bitcast.183, f32[4,1,8]{2,0,1:T(4,128)S(1)} %bitcast.182), channel_id=1, replica_groups=mesh['seq'=16,'head'=8] {'seq'}, use_global_device_ids=true, to_apply=%region_14.15 | all-reduce | flops 64 | bytes 512 | tf_op jit(solution)/shard_map/pmax | solution.py:118
  117.8 4.7 %fusion.3 = f32[4,8,128]{2,1,0:T(8,128)S(1)} fusion(bf16[4,16,512,128]{3,2,1,0:T(8,128)(2,1)} %bitcast.165, f32[4,8,16]{1,2,0:T(8,128)S(1)} %get-tuple-element.24, f32[4,8,16,512]{3,1,2,0:T(8,128)S(1)} %get-tuple-element.51, f32[4,8,16]{1,2,0:T(8,128)S(1)} %get-tuple-element.9, pred[4,16,512]{2,1,0:T(8,128)(4,1)S(1)} %broadcast_compare_fusion), kind=kOutput, calls=%fused_computation.5 | convolution fusion | flops 68022272 | bytes 9490432 | tf_op jit(solution)/shard_map/bkgnt,bntkd->bkgnd/dot_general | solution.py:95
  122.6 0.0 copy-start.2
  122.6 4.8 %fusion.2 = f32[4,8,128]{2,1,0:T(8,128)S(1)} fusion(bf16[4,16,512,128]{3,2,1,0:T(8,128)(2,1)} %bitcast.166, f32[4,8,16]{1,2,0:T(8,128)S(1)} %get-tuple-element.26, f32[4,8,16,512]{3,1,2,0:T(8,128)S(1)} %fusion.13, f32[4,8,16]{1,2,0:T(8,128)S(1)} %get-tuple-element.10, pred[4,16,512]{2,1,0:T(8,128)(4,1)S(1)} %broadcast_compare_fusion), kind=kOutput, calls=%fused_computation.4 | convolution fusion | flops 68022272 | bytes 9490432 | tf_op jit(solution)/shard_map/bkgnt,bntkd->bkgnd/dot_general | solution.py:95
  127.4 58.0 %all-reduce = (f32[4,1,8,128]{3,2,0,1:T(8,128)S(1)}, f32[4,1,8]{2,0,1:T(4,128)S(1)}, bf16[4,128]{1,0:T(4,128)(2,1)S(1)}, f32[4,128]{1,0:T(4,128)S(1)}, f32[4,1,8...) all-reduce(f32[4,1,8,128]{3,2,0,1:T(8,128)S(1)} %bitcast.170, ...), channel_id=1, replica_groups=mesh['seq'=16,'head'=8] {'seq'}, use_global_device_ids=true, to_apply=%region_18.19 | all-reduce | flops 9280 | bytes 73216 | tf_op jit(solution)/shard_map/psum | solution.py:123
  185.4 0.1 fusion.12
  185.6 0.2 fusion.7
  185.9 0.0 copy-done.2
  185.9 0.2 fusion.8
  186.1 0.8 copy.27
  186.9 0.0 reduce-scatter.4.cloned.1.call-update
  186.9 0.7 fusion.74
  187.6 0.6 maximum_bitcast_fusion
  188.2 57.7 %reduce-scatter.4.cloned.1.call-done = bf16[64,8]{1,0:T(8,128)(2,1)} async-done(((bf16[512,8]{1,0:T(8,128)(2,1)}), bf16[64,8]{1,0:T(8,128)(2,1)}) %reduce-scatter.4.cloned.1.call-update) | async-done | bytes 1040
  245.8 1.4 copy.28
  (18 shorter events, 0.2 us)
Async XLA Ops:
  7.2 1.2 copy-start
  7.2 78.0 %copy-start.3 = (f32[64]{0:T(128)S(1)}, f32[64]{0:T(128)}, u32[]{:S(2)}) copy-start(f32[64]{0:T(128)} %constant.73.clone) | copy-start | bytes 772
  7.2 78.0 %copy-start.4 = (f32[64]{0:T(128)S(1)}, f32[64]{0:T(128)}, u32[]{:S(2)}) copy-start(f32[64]{0:T(128)} %constant.74.clone) | copy-start | bytes 772
  7.2 238.6 %reduce-scatter.4.cloned.1.call-start = ((), (), s32[]{:S(2)}) async-start(), calls=%async_computation.1 | async-start | bytes 147456
  78.2 7.6 %copy-start.1 = (bf16[4,8192,128]{2,1,0:T(8,128)(2,1)S(1)}, bf16[4,8192,128]{2,1,0:T(8,128)(2,1)}, u32[]{:S(2)}) copy-start(bf16[4,8192,128]{2,1,0:T(8,128)(2,1)} %param.21) | copy-start | bytes 25165828
  122.6 63.3 %copy-start.2 = (bf16[1024,512]{1,0:T(8,128)(2,1)S(1)}, bf16[1024,512]{1,0:T(8,128)(2,1)}, u32[]{:S(2)}) copy-start(bf16[1024,512]{1,0:T(8,128)(2,1)} %param.20) | copy-start | bytes 3145732
Sparse Core Ops, SparseCore 0:
  187.1 58.7 reduce-scatter.3
where the time goes:
time: 256 us; the launch traced here: 254 us
  blocking collectives  149 us (58%)
  waiting for transfers between devices  57.7 us (23%)
  matrix products  24.5 us (10%)
  between operations  14.2 us (6%)
  other arithmetic  5.43 us (2%)
  local copies, waits for them, and re-layouts  3.39 us (1%)
    psum x1, blocking collectives, local(): lax.psum(projections(hidden[step_index]), 'seq')  62.3 us
    psum x1, blocking collectives, local(): summed, mixed = lax.psum((part_sum, part_out), 'seq')  58 us
    unnamed x2, waiting for transfers between devices  57.7 us
    pmax x1, blocking collectives, local(): global_top = lax.pmax(local_top, 'seq')  28.5 us
    dot_general x2, matrix products, local(): jnp.einsum('bkgnt,bntkd->bkgnd', weights, cached_values, preferred_elemen...  9.51 us
    dot_general x2, matrix products, local(): jnp.einsum('bkgd,bntkd->bkgnt', query_rows, cached_keys, preferred_elemen...  8.27 us
  transfers between devices with their start and end apart: 1, of which 1 were waited for; matrix products, arithmetic and copies ran while one was open for 0% of the time, Pallas kernels for 0%

commit v1 on v0

v1 whole, which is shorter than its diff:
```python
import functools

import jax
import jax.numpy as jnp
import numpy as np
from jax import lax
from jax.experimental import pallas as pl
from jax.experimental.pallas import tpu as pltpu
from jax.sharding import PartitionSpec as P

HEAD_WIDTH = 128
HALF = HEAD_WIDTH // 2
THETA = 500000.0
FILL = -1e30
F32 = jnp.float32
BF16 = jnp.bfloat16
VMEM = pltpu.MemorySpace.VMEM
SMEM = pltpu.MemorySpace.SMEM


def rotary_tables():
    exponent = np.arange(HALF) * 2.0 / HEAD_WIDTH
    inverse = THETA ** (-exponent)
    coarse = np.mod(1024.0 * inverse, 2.0 * np.pi)
    fine = np.concatenate([inverse, inverse])[None]
    coarse = np.concatenate([coarse, coarse])[None]
    return np.concatenate([fine, coarse]).astype(np.float32)


def project_kernel(copies, hidden_ref, wq_ref, wk_ref, wv_ref, out_ref):
    steps, batch, _ = hidden_ref.shape
    rows = jnp.concatenate([hidden_ref[s].astype(F32) for s in range(steps)], axis=0).astype(BF16)
    q_width = wq_ref.shape[1]
    kv_width = wk_ref.shape[1]
    query = jnp.dot(rows, wq_ref[...], preferred_element_type=F32).astype(BF16)
    key = jnp.dot(rows, wk_ref[...], preferred_element_type=F32).astype(BF16)
    value = jnp.dot(rows, wv_ref[...], preferred_element_type=F32).astype(BF16)
    for c in range(copies):
        out_ref[c, :, :q_width] = query
        out_ref[c, :, q_width : q_width + kv_width] = key
        out_ref[c, :, q_width + kv_width :] = value


def attend_kernel(
    steps, heads, chunk, copies, seq_ref, lengths_ref, sums_ref, cos_ref, sin_ref, keys_ref, values_ref,
    message_ref, new_keys_ref, new_values_ref, query_scr, scores_scr, out_scr,
):
    batch, context, width = keys_ref.shape
    rows = steps * batch
    group = steps * heads
    total = sums_ref[0].astype(F32)
    for d in range(1, sums_ref.shape[0]):
        total = total + sums_ref[d].astype(F32)
    cosine = cos_ref[...]
    sine = sin_ref[...]

    def rotate(x):
        return x * cosine + pltpu.roll(x, HALF, 1) * sine

    for h in range(heads):
        rotated = rotate(total[:, h * width : (h + 1) * width]) * (width**-0.5)
        for r in range(rows):
            s, b = divmod(r, batch)
            query_scr[b, s * heads + h : s * heads + h + 1, :] = rotated[r : r + 1]
    new_key = rotate(total[:, heads * width : (heads + 1) * width]).astype(BF16)
    new_value = total[:, (heads + 1) * width :]
    for s in range(steps):
        new_keys_ref[s] = new_key.astype(F32)[s * batch : (s + 1) * batch].astype(BF16)
        new_values_ref[s] = new_value[s * batch : (s + 1) * batch].astype(BF16)
    new_key = new_key.astype(F32)

    seq = seq_ref[0]
    owner = seq == 0
    sublane = lax.broadcasted_iota(jnp.int32, (group, width), 0)
    lane = lax.broadcasted_iota(jnp.int32, (group, width), 1)
    head_of = sublane % heads
    stat_lane = lane - head_of
    position = lax.broadcasted_iota(jnp.int32, (group, chunk), 1)
    row_step = lax.broadcasted_iota(jnp.int32, (group, 1), 0) // heads

    for b in range(batch):
        query = query_scr[b].astype(BF16)
        limit = lengths_ref[b] - seq * context
        top = jnp.full((group, chunk), FILL, F32)
        for start in range(0, context, chunk):
            scores = lax.dot_general(
                query, keys_ref[b, start : start + chunk, :], (((1,), (1,)), ((), ())),
                preferred_element_type=F32,
            )
            scores = jnp.where(position < limit - start, scores, FILL)
            scores_scr[:, start : start + chunk] = scores
            top = jnp.maximum(top, scores)
        top = jnp.max(top, axis=1, keepdims=True)
        query_wide = query.astype(F32)
        fresh = []
        for t in range(steps):
            row = t * batch + b
            score = jnp.sum(query_wide * new_key[row : row + 1], axis=1, keepdims=True)
            fresh.append(jnp.where(row_step >= t, score, FILL))
        fresh_top = functools.reduce(jnp.maximum, fresh)
        top = jnp.where(owner, jnp.maximum(top, fresh_top), top)
        top = top.astype(BF16).astype(F32)
        weight_sum = jnp.zeros((group, chunk), F32)
        out = jnp.zeros((group, width), F32)
        for start in range(0, context, chunk):
            weights = jnp.where(
                position < limit - start, jnp.exp(scores_scr[:, start : start + chunk] - top), 0.0
            ).astype(BF16)
            weight_sum = weight_sum + weights.astype(F32)
            out = out + jnp.dot(
                weights, values_ref[b, start : start + chunk, :], preferred_element_type=F32
            )
        weight_sum = jnp.sum(weight_sum, axis=1, keepdims=True)
        fresh_scale = jnp.where(owner, jnp.exp(fresh_top - jnp.where(owner, top, fresh_top)), 0.0)
        for t in range(steps):
            row = t * batch + b
            weight = jnp.where(row_step >= t, jnp.exp(fresh[t] - fresh_top), 0.0)
            weight = weight.astype(BF16).astype(F32) * fresh_scale
            weight_sum = weight_sum + weight
            out = out + weight * new_value[row : row + 1]
        sum_high = weight_sum.astype(BF16).astype(F32)
        sum_low = weight_sum - sum_high
        stats = jnp.where(
            stat_lane == 0, top,
            jnp.where(stat_lane == heads, sum_high, jnp.where(stat_lane == 2 * heads, sum_low, 0.0)),
        )
        for s in range(steps):
            r = s * batch + b
            out_scr[r : r + 1, heads * width :] = jnp.sum(
                stats[s * heads : (s + 1) * heads], axis=0, keepdims=True
            )
            for h in range(heads):
                out_scr[r : r + 1, h * width : (h + 1) * width] = out[s * heads + h : s * heads + h + 1]
    message = out_scr[...].astype(BF16)
    for c in range(copies):
        message_ref[c] = message


def combine_kernel(heads, head_ref, message_ref, w_out_ref, out_ref):
    devices, rows, _ = message_ref.shape
    width = HEAD_WIDTH
    stats = [message_ref[d, :, heads * width :].astype(F32) for d in range(devices)]
    top = functools.reduce(jnp.maximum, stats)
    total = jnp.zeros((rows, width), F32)
    factors = []
    lane = lax.broadcasted_iota(jnp.int32, (rows, width), 1)
    for d in range(devices):
        factor = jnp.exp(jnp.where(lane < heads, stats[d] - top, 0.0))
        sums = pltpu.roll(stats[d], width - heads, 1) + pltpu.roll(stats[d], width - 2 * heads, 1)
        total = total + factor * sums
        factors.append(factor)
    scale = 1.0 / jnp.where(lane < heads, total, 1.0)
    factors = [f * scale for f in factors]
    attended = []
    for h in range(heads):
        mixed = jnp.zeros((rows, width), F32)
        for d in range(devices):
            part = message_ref[d, :, h * width : (h + 1) * width].astype(F32)
            mixed = mixed + factors[d][:, h : h + 1] * part
        attended.append(mixed.astype(BF16))
    attended = jnp.concatenate(attended, axis=1)
    projected = jnp.dot(attended, w_out_ref[...], preferred_element_type=F32).astype(BF16)
    rank = head_ref[0] // 2
    ranks = out_ref.shape[0]
    for target in range(ranks):
        slot = lax.rem(target - rank + ranks, ranks)
        out_ref[slot] = projected[:, target * width : (target + 1) * width]


def in_vmem(x):
    return pltpu.with_memory_space_constraint(x, VMEM)


def gather_all(x, axis):
    return lax.all_to_all(x, axis, 0, 0, tiled=True)


def local(hidden, w_query, key_matrix, value_matrix, w_out, key_cache, value_cache, lengths):
    steps, batch, _ = hidden.shape
    rows = steps * batch
    width = HEAD_WIDTH
    heads = w_query.shape[1] // width
    devices = lax.axis_size("seq")
    seq = lax.axis_index("seq").astype(jnp.int32).reshape(1)
    head = lax.axis_index("head").astype(jnp.int32)
    whole = pl.BlockSpec(memory_space=VMEM)
    scalar = pl.BlockSpec(memory_space=SMEM)

    positions = (lengths[None, :] + jnp.arange(steps, dtype=jnp.int32)[:, None]).reshape(rows, 1)
    tables = jnp.asarray(rotary_tables())
    angles = (positions // 1024).astype(F32) * tables[1:2] + (positions % 1024).astype(F32) * tables[0:1]
    sign = jnp.asarray(np.where(np.arange(width) < HALF, -1.0, 1.0).astype(np.float32))[None]
    cosine = jnp.cos(angles)
    sine = jnp.sin(angles) * sign

    with jax.named_scope("projections"):
        partial_sums = pl.pallas_call(
            functools.partial(project_kernel, devices),
            out_shape=jax.ShapeDtypeStruct((devices, rows, (heads + 2) * width), BF16),
            in_specs=[whole] * 4,
            out_specs=whole,
        )(hidden, w_query, key_matrix, value_matrix)
    with jax.named_scope("sum_over_width"):
        sums = gather_all(partial_sums, "seq")
    with jax.named_scope("attention"):
        message, new_keys, new_values = pl.pallas_call(
            functools.partial(attend_kernel, steps, heads, 2048, devices),
            out_shape=(
                jax.ShapeDtypeStruct((devices, rows, (heads + 1) * width), BF16),
                jax.ShapeDtypeStruct((steps, batch, width), BF16),
                jax.ShapeDtypeStruct((steps, batch, width), BF16),
            ),
            in_specs=[scalar, scalar] + [whole] * 5,
            out_specs=(whole, whole, whole),
            scratch_shapes=[
                pltpu.VMEM((batch, steps * heads, width), F32),
                pltpu.VMEM((steps * heads, key_cache.shape[1]), F32),
                pltpu.VMEM((rows, (heads + 1) * width), F32),
            ],
            compiler_params=pltpu.CompilerParams(vmem_limit_bytes=8 * 2**20),
        )(seq, lengths, sums, cosine, sine, in_vmem(key_cache), in_vmem(value_cache))
    with jax.named_scope("combine"):
        messages = gather_all(message, "seq")
        ranks = lax.axis_size("head") // 2
        projected = pl.pallas_call(
            functools.partial(combine_kernel, heads),
            out_shape=jax.ShapeDtypeStruct((ranks, rows, width), BF16),
            in_specs=[scalar, whole, whole],
            out_specs=whole,
        )(head.reshape(1), in_vmem(messages), in_vmem(w_out))
    with jax.named_scope("sum_over_heads"):
        parts = [projected[0]]
        for d in range(1, ranks):
            route = [(2 * y + c, 2 * ((y + d) % ranks) + c) for y in range(ranks) for c in range(2)]
            parts.append(lax.ppermute(projected[d], "head", route))
        pair = sum(p.astype(F32) for p in parts)
        core = head % 2
        mine = jnp.where(core == 0, pair[:, :HALF], pair[:, HALF:])
        other = jnp.where(core == 0, pair[:, HALF:], pair[:, :HALF])
        other = lax.ppermute(other, "head", [(i, i ^ 1) for i in range(2 * ranks)])
        attn_out = (mine + other).astype(BF16).reshape(steps, batch, HALF)
    return attn_out, new_keys, new_values


def solution(mesh):
    in_specs = (
        P(None, None, "seq"),
        P("seq", "head"),
        P("seq", "head"),
        P("seq", "head"),
        P("head", "seq"),
        P(None, "seq", "head"),
        P(None, "seq", "head"),
        P(),
    )
    out_specs = (P(None, None, ("seq", "head")), P(None, None, "head"), P(None, None, "head"))
    return jax.shard_map(local, mesh=mesh, in_specs=in_specs, out_specs=out_specs, check_vma=False)
```

time: 256 us -> 60.1 us (0.23)
  blocking collectives: 149 us -> 0 us
  waiting for transfers between devices: 57.7 us -> 18.5 us
  matrix products: 24.5 us -> 0 us
  starting transfers between devices: 0.04 us -> 20.3 us
  between operations: 14.2 us -> 0.67 us
  Pallas kernels: 0 us -> 9.08 us
  local copies, waits for them, and re-layouts: 3.39 us -> 8.19 us
    psum x2 -> x0, blocking collectives: 120 us -> none  [the longest x1 62.3 us: local(): lax.psum(projections(hidden[step_index]), 'seq')]
    unnamed x2 -> x0, waiting for transfers between devices: 57.7 us -> none
    pmax x1 -> x0, blocking collectives: 28.5 us -> none  [local(): global_top = lax.pmax(local_top, 'seq')]
    dot_general x14 -> x0, matrix products: 24.5 us -> none  [the longest x2 9.51 us: local(): jnp.einsum('bkgnt,bntkd->bkgnd', weights, cached_values, preferred_elemen...]
    all_to_all x0 -> x2, waiting for transfers between devices: none -> 14.8 us  [gather_all(): return lax.all_to_all(x, axis, 0, 0, tiled=True)]
    all_to_all x0 -> x2, starting transfers between devices: none -> 12 us  [gather_all(): return lax.all_to_all(x, axis, 0, 0, tiled=True)]
    pallas_call x0 -> x3, Pallas kernels: none -> 9.08 us  [the longest x1 5.76 us: local(): pl.pallas_call(functools.partial(attend_kernel, steps, heads, 2048, devic...]
    ppermute x0 -> x4, starting transfers between devices: none -> 8.34 us  [the longest x1 4.56 us: local(): other = lax.ppermute(other, 'head', [(i, i ^ 1) for i in range(2 * ranks)])]
  transfers between devices with their start and end apart: 1 -> 6, of which waited for: 1 -> 5; matrix products, arithmetic and copies ran while one was open for 0% -> 3% of each run, Pallas kernels for 0% -> 0%
where the time goes in v1:
time: 60.1 us; the launch traced here: 59.6 us
  starting transfers between devices  20.3 us (34%)
  waiting for transfers between devices  18.5 us (31%)
  Pallas kernels  9.08 us (15%)
  local copies, waits for them, and re-layouts  8.19 us (14%)
  other arithmetic  2.88 us (5%)
  between operations  0.67 us (1%)
    all_to_all x2, waiting for transfers between devices, gather_all(): return lax.all_to_all(x, axis, 0, 0, tiled=True)  14.8 us
    all_to_all x2, starting transfers between devices, gather_all(): return lax.all_to_all(x, axis, 0, 0, tiled=True)  12 us
    unnamed x8, local copies, waits for them, and re-layouts  7.42 us
    pallas_call x1, Pallas kernels, local(): pl.pallas_call(functools.partial(attend_kernel, steps, heads, 2048, devic...  5.76 us
    ppermute x1, starting transfers between devices, local(): other = lax.ppermute(other, 'head', [(i, i ^ 1) for i in range(2 * ranks)])  4.56 us
    ppermute x3, starting transfers between devices, local(): parts.append(lax.ppermute(projected[d], 'head', route))  3.77 us
    ppermute x3, waiting for transfers between devices, local(): parts.append(lax.ppermute(projected[d], 'head', route))  2.95 us
    pallas_call x1, Pallas kernels, local(): pl.pallas_call(functools.partial(project_kernel, devices), out_shape=jax....  2.29 us
  transfers between devices with their start and end apart: 6, of which 5 were waited for; matrix products, arithmetic and copies ran while one was open for 3% of the time, Pallas kernels for 0%

profile of v1, /device:TPU:1, one launch (start us, length us, event | category | flops | bytes accessed | tf_op | source)
XLA Modules:
  0.0 59.6 jit_solution(2090100848087931038)
XLA Ops:
  0.6 2.3 %projections.1 = bf16[16,8,1280]{2,1,0:T(8,128)(2,1)} custom-call(bf16[2,4,512]{2,1,0:T(4,128)(2,1)} %hidden_ref.1, bf16[512,1024]{1,0:T(8,128)(2,1)} %wq_ref.1, bf16[512,128]{1,0:T(8,128)(2,1)} %wk_ref.1, bf16[512,128]{1,0:T(8,128)(2,1)} %wv_ref.1), custom_call_target="tpu_custom_call" | custom-call | tf_op jit(solution)/shard_map/projections/pallas_call | solution.py:197
  2.9 8.4 %all-to-all-start = ((bf16[16,8,1280]{2,1,0:T(8,128)(2,1)}), bf16[16,8,1280]{2,1,0:T(8,128)(2,1)S(1)}, u32[]{:S(2)}, u32[]{:S(2)}) async-start(bf16[16,8,1280]{2,1,0:T(8,128)(2,1)} %projections.1), calls=%async_computation | async-start | bytes 655360 | tf_op jit(solution)/shard_map/sum_over_width/all_to_all | solution.py:175
  11.4 0.7 %iota_add_fusion = s32[2,4]{1,0:T(2,128)S(1)} fusion(s32[4]{0:T(128)} %lengths_ref.1), kind=kLoop, calls=%fused_computation.17 | loop fusion | flops 8 | bytes 48 | tf_op jit(solution)/shard_map/add | solution.py:189
  12.0 0.1 add.77
  12.1 0.8 %sine_multiply_fusion = (f32[8,128]{1,0:T(8,128)S(1)}, f32[8,128]{1,0:T(8,128)S(1)}) fusion(f32[128]{0:T(128)} %constant.54.clone, f32[128]{0:T(128)} %constant.58, f32[8]{0:T(128)S(1)} %get-tuple-element.15, f32[128]{0:T(128)} %constant.56, f32[8]{0:T(128)S(1)} %get-tuple-element.14), kind=kLoop, calls=%fused_computation.4 | loop fusion | flops 4096 | bytes 9792 | tf_op jit(solution)/shard_map/mul | solution.py:194
  12.9 6.9 %all-to-all-done.sums_ref = bf16[16,8,1280]{2,1,0:T(8,128)(2,1)S(1)} async-done(((bf16[16,8,1280]{2,1,0:T(8,128)(2,1)}), bf16[16,8,1280]{2,1,0:T(8,128)(2,1)S(1)}, u32[]{:S(2)}, u32[]{:S(2)}) %all-to-all-start) | async-done | bytes 327712 | tf_op jit(solution)/shard_map/sum_over_width/all_to_all | solution.py:175
  19.8 0.0 copy-start
  19.8 3.4 %copy-done = bf16[4,8192,128]{2,1,0:T(8,128)(2,1)S(1)} copy-done((bf16[4,8192,128]{2,1,0:T(8,128)(2,1)S(1)}, bf16[4,8192,128]{2,1,0:T(8,128)(2,1)}, u32[]{:S(2)}) %copy-start) | copy-done | bytes 8388632
  23.2 0.0 copy-start.1
  23.2 3.4 %copy-done.1 = bf16[4,8192,128]{2,1,0:T(8,128)(2,1)S(1)} copy-done((bf16[4,8192,128]{2,1,0:T(8,128)(2,1)S(1)}, bf16[4,8192,128]{2,1,0:T(8,128)(2,1)}, u32[]{:S(2)}) %copy-start.1) | copy-done | bytes 8388632
  26.6 0.0 copy-start.3
  26.6 0.7 %copy-done.3 = s32[4]{0:T(128)S(1)} copy-done((s32[4]{0:T(128)S(1)}, s32[4]{0:T(128)}, u32[]{:S(2)}) %copy-start.3) | copy-done | bytes 40
  27.2 0.0 copy-start.2
  27.2 5.8 %attention.1 = (bf16[16,8,1152]{2,1,0:T(8,128)(2,1)}, bf16[2,4,128]{2,1,0:T(4,128)(2,1)}, bf16[2,4,128]{2,1,0:T(4,128)(2,1)}) custom-call(s32[1]{0:T(128)} %bitcast.1.seq_ref, s32[4]{0:T(128)S(1)} %copy-done.3, bf16[16,8,1280]{2,1,0:T(8,128)(2,1)S(1)} %all-to-all-done.sums_ref, f32[8,128]{1,0:T(8,128)S(1)} %get-tuple-element.13.cos_ref, ...), custom_call_target="tpu_custom_call" | custom-call | tf_op jit(solution)/shard_map/attention/pallas_call | solution.py:206
  33.0 3.5 %all-to-all-start.1 = ((bf16[16,8,1152]{2,1,0:T(8,128)(2,1)}), bf16[16,8,1152]{2,1,0:T(8,128)(2,1)S(1)}, u32[]{:S(2)}, u32[]{:S(2)}) async-start(bf16[16,8,1152]{2,1,0:T(8,128)(2,1)} %get-tuple-element.6), calls=%async_computation.1 | async-start | bytes 589824 | tf_op jit(solution)/shard_map/combine/all_to_all | solution.py:175
  36.6 7.8 %all-to-all-done.1.message_ref = bf16[16,8,1152]{2,1,0:T(8,128)(2,1)S(1)} async-done(((bf16[16,8,1152]{2,1,0:T(8,128)(2,1)}), bf16[16,8,1152]{2,1,0:T(8,128)(2,1)S(1)}, u32[]{:S(2)}, u32[]{:S(2)}) %all-to-all-start.1) | async-done | bytes 294944 | tf_op jit(solution)/shard_map/combine/all_to_all | solution.py:175
  44.4 0.0 copy-done.2
  44.4 1.0 %combine.1 = bf16[4,8,128]{2,1,0:T(8,128)(2,1)} custom-call(s32[1]{0:T(128)} %bitcast.head_ref, bf16[16,8,1152]{2,1,0:T(8,128)(2,1)S(1)} %all-to-all-done.1.message_ref, bf16[1024,512]{1,0:T(8,128)(2,1)S(1)} %copy-done.2), custom_call_target="tpu_custom_call" | custom-call | tf_op jit(solution)/shard_map/combine/pallas_call | solution.py:225
  45.4 0.7 %slice_bitcast_fusion.2 = (bf16[8,128]{1,0:T(8,128)(2,1)S(1)}, bf16[8,128]{1,0:T(8,128)(2,1)S(1)}, bf16[8,128]{1,0:T(8,128)(2,1)S(1)}) fusion(bf16[4,8,128]{2,1,0:T(8,128)(2,1)} %combine.1), kind=kLoop, calls=%fused_computation.10 | loop fusion | bytes 12288 | tf_op jit(solution)/shard_map/sum_over_heads/squeeze | solution.py:235
  46.1 2.7 %collective-permute-start.2 = (bf16[8,128]{1,0:T(8,128)(2,1)S(1)}, bf16[8,128]{1,0:T(8,128)(2,1)S(1)}, u32[]{:S(2)}, u32[]{:S(2)}) collective-permute-start(bf16[8,128]{1,0:T(8,128)(2,1)S(1)} %get-tuple-element.10), channel_id=1, source_target_pairs={{0,6},{1,7},{2,0},{3,1},{4,2},{5,3},{6,4},{7,5},{8,14},{9,15},{10,... | collective-permute-start | bytes 6152 | tf_op jit(solution)/shard_map/sum_over_heads/ppermute | solution.py:235
  48.9 0.3 collective-permute-start.1
  49.2 0.7 %collective-permute-start = (bf16[8,128]{1,0:T(8,128)(2,1)S(1)}, bf16[8,128]{1,0:T(8,128)(2,1)S(1)}, u32[]{:S(2)}, u32[]{:S(2)}) collective-permute-start(bf16[8,128]{1,0:T(8,128)(2,1)S(1)} %get-tuple-element.9), channel_id=1, source_target_pairs={{0,2},{1,3},{2,4},{3,5},{4,6},{5,7},{6,0},{7,1},{8,10},{9,11},{10,... | collective-permute-start | bytes 6152 | tf_op jit(solution)/shard_map/sum_over_heads/ppermute | solution.py:235
  49.9 0.0 collective-permute-done.2
  49.9 2.9 %collective-permute-done.1 = bf16[8,128]{1,0:T(8,128)(2,1)S(1)} collective-permute-done((bf16[8,128]{1,0:T(8,128)(2,1)S(1)}, bf16[8,128]{1,0:T(8,128)(2,1)S(1)}, u32[]{:S(2)}, u32[]{:S(2)}) %collective-permute-start.1) | collective-permute-done | bytes 2080 | tf_op jit(solution)/shard_map/sum_over_heads/ppermute | solution.py:235
  52.8 0.1 collective-permute-done
  52.9 0.7 %fusion.1 = f32[8,128]{1,0:T(8,128)S(1)} fusion(bf16[8,128]{1,0:T(8,128)(2,1)S(1)} %collective-permute-done.2, bf16[8,128]{1,0:T(8,128)(2,1)S(1)} %collective-permute-done.1, bf16[8,128]{1,0:T(8,128)(2,1)S(1)} %collective-permute-done, bf16[4,8,128]{2,1,0:T(8,128)(2,1)} %combine.1), kind=kLoop, calls=%fused_computation.2 | loop fusion | flops 7168 | bytes 12288 | tf_op jit(solution)/shard_map/sum_over_heads/add | solution.py:236
  53.5 0.1 slice_select_fusion
  53.6 4.6 %collective-permute-start.3 = (f32[8,64]{1,0:T(8,128)S(1)}, f32[8,64]{1,0:T(8,128)S(1)}, u32[]{:S(2)}, u32[]{:S(2)}) collective-permute-start(f32[8,64]{1,0:T(8,128)S(1)} %slice_select_fusion), channel_id=1, source_target_pairs={{0,1},{1,0},{2,3},{3,2},{4,5},{5,4},{6,7},{7,6},{8,9},{9,8},{10,11... | collective-permute-start | bytes 6152 | tf_op jit(solution)/shard_map/sum_over_heads/ppermute | solution.py:240
  58.2 0.8 %collective-permute-done.3 = f32[8,64]{1,0:T(8,128)S(1)} collective-permute-done((f32[8,64]{1,0:T(8,128)S(1)}, f32[8,64]{1,0:T(8,128)S(1)}, u32[]{:S(2)}, u32[]{:S(2)}) %collective-permute-start.3) | collective-permute-done | bytes 2080 | tf_op jit(solution)/shard_map/sum_over_heads/ppermute | solution.py:240
  59.0 0.7 %add_convert_fusion = bf16[8,64]{1,0:T(8,128)(2,1)} fusion(f32[8,64]{1,0:T(8,128)S(1)} %collective-permute-done.3, f32[8,128]{1,0:T(8,128)S(1)} %fusion.1, pred[]{:T(512)S(6)} %eq.8), kind=kLoop, calls=%fused_computation.3 | loop fusion | flops 1536 | bytes 7169 | tf_op jit(solution)/shard_map/sum_over_heads/convert_element_type | solution.py:241
  (1 shorter events, 0.0 us)
Async XLA Ops:
  2.9 16.9 %all-to-all-start = ((bf16[16,8,1280]{2,1,0:T(8,128)(2,1)}), bf16[16,8,1280]{2,1,0:T(8,128)(2,1)S(1)}, u32[]{:S(2)}, u32[]{:S(2)}) async-start(bf16[16,8,1280]{2,1,0:T(8,128)(2,1)} %projections.1), calls=%async_computation | async-start | bytes 655360 | tf_op jit(solution)/shard_map/sum_over_width/all_to_all | solution.py:175
  19.8 3.4 %copy-start = (bf16[4,8192,128]{2,1,0:T(8,128)(2,1)S(1)}, bf16[4,8192,128]{2,1,0:T(8,128)(2,1)}, u32[]{:S(2)}) copy-start(bf16[4,8192,128]{2,1,0:T(8,128)(2,1)} %keys_ref.1) | copy-start | bytes 25165828
  23.2 3.4 %copy-start.1 = (bf16[4,8192,128]{2,1,0:T(8,128)(2,1)S(1)}, bf16[4,8192,128]{2,1,0:T(8,128)(2,1)}, u32[]{:S(2)}) copy-start(bf16[4,8192,128]{2,1,0:T(8,128)(2,1)} %values_ref.1) | copy-start | bytes 25165828
  26.6 0.7 %copy-start.3 = (s32[4]{0:T(128)S(1)}, s32[4]{0:T(128)}, u32[]{:S(2)}) copy-start(s32[4]{0:T(128)} %lengths_ref.1) | copy-start | bytes 52
  27.2 17.2 %copy-start.2 = (bf16[1024,512]{1,0:T(8,128)(2,1)S(1)}, bf16[1024,512]{1,0:T(8,128)(2,1)}, u32[]{:S(2)}) copy-start(bf16[1024,512]{1,0:T(8,128)(2,1)} %w_out_ref.1) | copy-start | bytes 3145732
  33.0 11.4 %all-to-all-start.1 = ((bf16[16,8,1152]{2,1,0:T(8,128)(2,1)}), bf16[16,8,1152]{2,1,0:T(8,128)(2,1)S(1)}, u32[]{:S(2)}, u32[]{:S(2)}) async-start(bf16[16,8,1152]{2,1,0:T(8,128)(2,1)} %get-tuple-element.6), calls=%async_computation.1 | async-start | bytes 589824 | tf_op jit(solution)/shard_map/combine/all_to_all | solution.py:175
  46.1 3.8 %collective-permute-start.2 = (bf16[8,128]{1,0:T(8,128)(2,1)S(1)}, bf16[8,128]{1,0:T(8,128)(2,1)S(1)}, u32[]{:S(2)}, u32[]{:S(2)}) collective-permute-start(bf16[8,128]{1,0:T(8,128)(2,1)S(1)} %get-tuple-element.10), channel_id=1, source_target_pairs={{0,6},{1,7},{2,0},{3,1},{4,2},{5,3},{6,4},{7,5},{8,14},{9,15},{10,... | collective-permute-start | bytes 6152 | tf_op jit(solution)/shard_map/sum_over_heads/ppermute | solution.py:235
  48.9 3.9 %collective-permute-start.1 = (bf16[8,128]{1,0:T(8,128)(2,1)S(1)}, bf16[8,128]{1,0:T(8,128)(2,1)S(1)}, u32[]{:S(2)}, u32[]{:S(2)}) collective-permute-start(bf16[8,128]{1,0:T(8,128)(2,1)S(1)} %get-tuple-element.11), channel_id=1, source_target_pairs={{0,4},{1,5},{2,6},{3,7},{4,0},{5,1},{6,2},{7,3},{8,12},{9,13},{10,... | collective-permute-start | bytes 6152 | tf_op jit(solution)/shard_map/sum_over_heads/ppermute | solution.py:235
  49.2 3.6 %collective-permute-start = (bf16[8,128]{1,0:T(8,128)(2,1)S(1)}, bf16[8,128]{1,0:T(8,128)(2,1)S(1)}, u32[]{:S(2)}, u32[]{:S(2)}) collective-permute-start(bf16[8,128]{1,0:T(8,128)(2,1)S(1)} %get-tuple-element.9), channel_id=1, source_target_pairs={{0,2},{1,3},{2,4},{3,5},{4,6},{5,7},{6,0},{7,1},{8,10},{9,11},{10,... | collective-permute-start | bytes 6152 | tf_op jit(solution)/shard_map/sum_over_heads/ppermute | solution.py:235
  53.6 5.4 %collective-permute-start.3 = (f32[8,64]{1,0:T(8,128)S(1)}, f32[8,64]{1,0:T(8,128)S(1)}, u32[]{:S(2)}, u32[]{:S(2)}) collective-permute-start(f32[8,64]{1,0:T(8,128)S(1)} %slice_select_fusion), channel_id=1, source_target_pairs={{0,1},{1,0},{2,3},{3,2},{4,5},{5,4},{6,7},{7,6},{8,9},{9,8},{10,11... | collective-permute-start | bytes 6152 | tf_op jit(solution)/shard_map/sum_over_heads/ppermute | solution.py:240

commit v2 on v1

v2 whole, which is shorter than its diff:
```python
import functools

import jax
import jax.numpy as jnp
import numpy as np
from jax import lax
from jax.experimental import pallas as pl
from jax.experimental.pallas import tpu as pltpu
from jax.sharding import PartitionSpec as P

HEAD_WIDTH = 128
HALF = HEAD_WIDTH // 2
THETA = 500000.0
FILL = -1e30
F32 = jnp.float32
BF16 = jnp.bfloat16
VMEM = pltpu.MemorySpace.VMEM


def rotary_tables():
    exponent = np.arange(HALF) * 2.0 / HEAD_WIDTH
    inverse = THETA ** (-exponent)
    coarse = np.mod(1024.0 * inverse, 2.0 * np.pi)
    fine = np.concatenate([inverse, inverse])[None]
    coarse = np.concatenate([coarse, coarse])[None]
    sign = np.where(np.arange(HEAD_WIDTH) < HALF, -1.0, 1.0)[None]
    return np.concatenate([fine, coarse, sign]).astype(np.float32)


def note_kernel(x_ref, o_ref):
    o_ref[...] = x_ref[...]


def project_kernel(
    steps, constants_hbm, lengths_hbm, hidden_hbm, wk_hbm, wv_hbm, wq_hbm, _, __, out_ref, tables_ref,
    constants_ref, lengths_ref, hidden_ref, wk_ref, wv_ref, wq_ref, sems,
):
    pairs = [
        (constants_hbm, constants_ref), (lengths_hbm, lengths_ref), (hidden_hbm, hidden_ref),
        (wk_hbm, wk_ref), (wv_hbm, wv_ref), (wq_hbm, wq_ref),
    ]
    copies = [pltpu.make_async_copy(src, dst, sems.at[i]) for i, (src, dst) in enumerate(pairs)]
    for copy in copies:
        copy.start()
    copies[0].wait()
    copies[1].wait()
    batch = lengths_ref.shape[0]
    rows = steps * batch
    width = constants_ref.shape[1]
    sublane = lax.broadcasted_iota(jnp.int32, (rows, width), 0)
    position = jnp.zeros((rows, width), jnp.int32)
    for r in range(rows):
        s, b = divmod(r, batch)
        position = jnp.where(sublane == r, lengths_ref[b] + s, position)
    upper = jnp.right_shift(position, 10).astype(F32)
    lower = jnp.bitwise_and(position, 1023).astype(F32)
    angles = upper * constants_ref[1:2, :] + lower * constants_ref[0:1, :]
    tables_ref[:rows, :] = jnp.cos(angles)
    tables_ref[rows : 2 * rows, :] = jnp.sin(angles) * constants_ref[2:3, :]
    tables_ref[2 * rows :, :] = position.astype(F32)
    copies[2].wait()
    hidden = jnp.concatenate([hidden_ref[s].astype(F32) for s in range(steps)], axis=0).astype(BF16)
    q_width = wq_ref.shape[1]
    kv_width = wk_ref.shape[1]
    copies[3].wait()
    key = jnp.dot(hidden, wk_ref[...], preferred_element_type=F32)
    out_ref[:, q_width : q_width + kv_width] = key.astype(BF16)
    copies[4].wait()
    value = jnp.dot(hidden, wv_ref[...], preferred_element_type=F32)
    out_ref[:, q_width + kv_width :] = value.astype(BF16)
    copies[5].wait()
    query = jnp.dot(hidden, wq_ref[...], preferred_element_type=F32)
    out_ref[:, :q_width] = query.astype(BF16)


def fetch_kernel(first, source_ref, target_ref, sem):
    batch = target_ref.shape[0]
    copies = [
        pltpu.make_async_copy(source_ref.at[first + b], target_ref.at[b], sem.at[b]) for b in range(batch)
    ]
    for copy in copies:
        copy.start()
    for copy in copies:
        copy.wait()


def attend_kernel(
    steps, heads, chunk, copies, tables_ref, sum0_ref, sum1_ref, sum2_ref, sum3_ref, *refs
):
    *keys_refs, values_ref, message_ref, new_keys_hbm, new_values_hbm = refs[:-8]
    query_scr, scores_scr, out_scr, value_buf, new_keys_ref, new_values_ref, value_sems, new_sems = refs[-8:]
    batch, context, width = values_ref.shape
    each = batch // len(keys_refs)

    def fetch(b):
        return pltpu.make_async_copy(values_ref.at[b], value_buf.at[b], value_sems.at[b])

    rows = steps * batch
    group = steps * heads
    total = sum0_ref[...].astype(F32)
    for part_ref in (sum1_ref, sum2_ref, sum3_ref):
        total = total + part_ref[...].astype(F32)
    cosine = tables_ref[:rows]
    sine = tables_ref[rows : 2 * rows]

    def rotate(x):
        return x * cosine + pltpu.roll(x, HALF, 1) * sine

    for h in range(heads):
        rotated = rotate(total[:, h * width : (h + 1) * width]) * (width**-0.5)
        for r in range(rows):
            s, b = divmod(r, batch)
            query_scr[b, s * heads + h : s * heads + h + 1, :] = rotated[r : r + 1]
    new_key = rotate(total[:, heads * width : (heads + 1) * width]).astype(BF16).astype(F32)
    new_value = total[:, (heads + 1) * width :]
    for s in range(steps):
        new_keys_ref[s] = new_key[s * batch : (s + 1) * batch].astype(BF16)
        new_values_ref[s] = new_value[s * batch : (s + 1) * batch].astype(BF16)
    new_copies = [
        pltpu.make_async_copy(new_keys_ref, new_keys_hbm, new_sems.at[0]),
        pltpu.make_async_copy(new_values_ref, new_values_hbm, new_sems.at[1]),
    ]
    for copy in new_copies:
        copy.start()

    seq = lax.axis_index("seq")
    first = seq * context
    owner = seq == 0
    sublane = lax.broadcasted_iota(jnp.int32, (group, width), 0)
    lane = lax.broadcasted_iota(jnp.int32, (group, width), 1)
    stat_lane = lane - sublane % heads
    position = lax.broadcasted_iota(jnp.int32, (group, chunk), 1)
    row_step = lax.broadcasted_iota(jnp.int32, (group, 1), 0) // heads

    tops = []
    for b in range(batch):
        query = query_scr[b].astype(BF16)
        keys_ref = keys_refs[b // each]
        limit = tables_ref[2 * rows + b : 2 * rows + b + 1, :1].astype(jnp.int32) - first
        top = jnp.full((group, chunk), FILL, F32)
        for start in range(0, context, chunk):
            scores = lax.dot_general(
                query, keys_ref[b % each, start : start + chunk, :], (((1,), (1,)), ((), ())),
                preferred_element_type=F32,
            )
            scores = jnp.where(position < limit - start, scores, FILL)
            scores_scr[b, :, start : start + chunk] = scores
            top = jnp.maximum(top, scores)
        tops.append(jnp.max(top, axis=1, keepdims=True))
    for b in range(batch):
        limit = tables_ref[2 * rows + b : 2 * rows + b + 1, :1].astype(jnp.int32) - first
        top = tops[b]
        query_wide = query_scr[b].astype(BF16).astype(F32)
        fresh = []
        for t in range(steps):
            row = t * batch + b
            score = jnp.sum(query_wide * new_key[row : row + 1], axis=1, keepdims=True)
            fresh.append(jnp.where(row_step >= t, score, FILL))
        fresh_top = functools.reduce(jnp.maximum, fresh)
        top = jnp.where(owner, jnp.maximum(top, fresh_top), top)
        top = top.astype(BF16).astype(F32)
        weight_sum = jnp.zeros((group, chunk), F32)
        out = jnp.zeros((group, width), F32)
        for start in range(0, context, chunk):
            weights = jnp.where(
                position < limit - start, jnp.exp(scores_scr[b, :, start : start + chunk] - top), 0.0
            ).astype(BF16)
            weight_sum = weight_sum + weights.astype(F32)
            out = out + jnp.dot(
                weights, values_ref[b, start : start + chunk, :], preferred_element_type=F32
            )
        weight_sum = jnp.sum(weight_sum, axis=1, keepdims=True)
        fresh_scale = jnp.where(owner, jnp.exp(fresh_top - jnp.where(owner, top, fresh_top)), 0.0)
        for t in range(steps):
            row = t * batch + b
            weight = jnp.where(row_step >= t, jnp.exp(fresh[t] - fresh_top), 0.0)
            weight = weight.astype(BF16).astype(F32) * fresh_scale
            weight_sum = weight_sum + weight
            out = out + weight * new_value[row : row + 1]
        sum_high = weight_sum.astype(BF16).astype(F32)
        sum_low = weight_sum - sum_high
        stats = jnp.where(
            stat_lane == 0, top,
            jnp.where(stat_lane == heads, sum_high, jnp.where(stat_lane == 2 * heads, sum_low, 0.0)),
        )
        for s in range(steps):
            r = s * batch + b
            out_scr[r : r + 1, heads * width :] = jnp.sum(
                stats[s * heads : (s + 1) * heads], axis=0, keepdims=True
            )
            for h in range(heads):
                out_scr[r : r + 1, h * width : (h + 1) * width] = out[s * heads + h : s * heads + h + 1]
    message = out_scr[...].astype(BF16)
    for c in range(copies):
        message_ref[c] = message
    for copy in new_copies:
        copy.wait()


def combine_kernel(heads, message_ref, w_out_ref, mine_ref, other_ref):
    devices, rows, _ = message_ref.shape
    width = HEAD_WIDTH
    stats = [message_ref[d, :, heads * width :].astype(F32) for d in range(devices)]
    top = functools.reduce(jnp.maximum, stats)
    total = jnp.zeros((rows, width), F32)
    factors = []
    lane = lax.broadcasted_iota(jnp.int32, (rows, width), 1)
    for d in range(devices):
        factor = jnp.exp(jnp.where(lane < heads, stats[d] - top, 0.0))
        sums = pltpu.roll(stats[d], width - heads, 1) + pltpu.roll(stats[d], width - 2 * heads, 1)
        total = total + factor * sums
        factors.append(factor)
    scale = 1.0 / jnp.where(lane < heads, total, 1.0)
    factors = [f * scale for f in factors]
    attended = []
    for h in range(heads):
        mixed = jnp.zeros((rows, width), F32)
        for d in range(devices):
            part = message_ref[d, :, h * width : (h + 1) * width].astype(F32)
            mixed = mixed + factors[d][:, h : h + 1] * part
        attended.append(mixed.astype(BF16))
    attended = jnp.concatenate(attended, axis=1)
    projected = jnp.dot(attended, w_out_ref[...], preferred_element_type=F32)
    head = lax.axis_index("head")
    rank = head // 2
    first_core = head % 2 == 0
    for target in range(mine_ref.shape[0]):
        block = projected[:, target * width : (target + 1) * width]
        swapped = pltpu.roll(block, HALF, 1)
        slot = jnp.bitwise_xor(rank, target)
        mine_ref[slot] = jnp.where(first_core, block, swapped)[:, :HALF].astype(BF16)
        other_ref[slot] = jnp.where(first_core, swapped, block)[:, :HALF].astype(BF16)


def in_vmem(x):
    return pltpu.with_memory_space_constraint(x, VMEM)


def exchange_routes(count, inner, axis_inner, order=(1, 3, 2)):
    routes = []
    for d in order:
        pairs = []
        for i in range(count):
            for j in range(inner):
                pairs.append((i * inner + j, (i ^ d) * inner + j) if axis_inner else (j * count + i, j * count + (i ^ d)))
        routes.append(pairs)
    return routes


def in_hbm(x):
    return pltpu.with_memory_space_constraint(x, pltpu.MemorySpace.HBM)


def gather_all(x, axis):
    return lax.all_to_all(x, axis, 0, 0, tiled=True)


def local(hidden, w_query, key_matrix, value_matrix, w_out, key_cache, value_cache, lengths):
    steps, batch, _ = hidden.shape
    rows = steps * batch
    width = HEAD_WIDTH
    heads = w_query.shape[1] // width
    devices = lax.axis_size("seq")
    whole = pl.BlockSpec(memory_space=VMEM)
    anywhere = pl.BlockSpec(memory_space=pl.ANY)

    with jax.named_scope("projections"):
        operands = (jnp.asarray(rotary_tables()), lengths, hidden, key_matrix, value_matrix, w_query)
        buffers = [
            (pltpu.SMEM if x.ndim == 1 else pltpu.VMEM)(x.shape, x.dtype) for x in operands
        ]
        partial_sums, tables = pl.pallas_call(
            functools.partial(project_kernel, steps),
            out_shape=(
                jax.ShapeDtypeStruct((rows, (heads + 2) * width), BF16),
                jax.ShapeDtypeStruct((3 * rows, width), F32),
            ),
            in_specs=[anywhere] * 8,
            out_specs=(whole, whole),
            scratch_shapes=buffers + [pltpu.SemaphoreType.DMA((6,))],
            compiler_params=pltpu.CompilerParams(vmem_limit_bytes=4 * 2**20),
        )(*[in_hbm(x) for x in operands], in_hbm(key_cache), in_hbm(value_cache))
    def note(x):
        return pl.pallas_call(
            note_kernel, out_shape=jax.ShapeDtypeStruct(x.shape, x.dtype), in_specs=[whole], out_specs=whole,
            cost_estimate=pl.CostEstimate(flops=0, bytes_accessed=16800000, transcendentals=0),
            compiler_params=pltpu.CompilerParams(vmem_limit_bytes=2**20),
        )(x)

    with jax.named_scope("sum_over_width"):
        along_x = exchange_routes(4, devices // 4, False)
        along_z = exchange_routes(4, devices // 4, True)
        sums = [partial_sums] + [lax.ppermute(partial_sums, "seq", route) for route in along_x]
        sums = functools.reduce(jnp.add, [x.astype(F32) for x in sums]).astype(BF16)
        sums = [sums] + [lax.ppermute(sums, "seq", route) for route in along_z]
    with jax.named_scope("attention"):
        message, new_keys, new_values = pl.pallas_call(
            functools.partial(attend_kernel, steps, heads, 2048, devices),
            out_shape=(
                jax.ShapeDtypeStruct((devices, rows, (heads + 1) * width), BF16),
                jax.ShapeDtypeStruct((steps, batch, width), BF16),
                jax.ShapeDtypeStruct((steps, batch, width), BF16),
            ),
            in_specs=[whole] * 7,
            out_specs=(whole, anywhere, anywhere),
            scratch_shapes=[
                pltpu.VMEM((batch, steps * heads, width), F32),
                pltpu.VMEM((batch, steps * heads, key_cache.shape[1]), F32),
                pltpu.VMEM((rows, (heads + 1) * width), F32),
                pltpu.VMEM((1,8,128), BF16),
                pltpu.VMEM((steps, batch, width), BF16),
                pltpu.VMEM((steps, batch, width), BF16),
                pltpu.SemaphoreType.DMA((batch,)),
                pltpu.SemaphoreType.DMA((2,)),
            ],
            compiler_params=pltpu.CompilerParams(vmem_limit_bytes=16 * 2**20),
        )(tables, *sums, in_vmem(key_cache), in_vmem(value_cache))
    with jax.named_scope("combine"):
        messages = gather_all(message, "seq")
        ranks = lax.axis_size("head") // 2
        part = jax.ShapeDtypeStruct((ranks, rows, HALF), BF16)
        mine, other = pl.pallas_call(
            functools.partial(combine_kernel, heads),
            out_shape=(part, part),
            in_specs=[whole, whole],
            out_specs=(whole, whole),
            compiler_params=pltpu.CompilerParams(vmem_limit_bytes=4 * 2**20),
        )(in_vmem(messages), in_vmem(w_out))
    with jax.named_scope("sum_over_heads"):
        other = lax.ppermute(other, "head", [(i, i ^ 1) for i in range(2 * ranks)])
        pair = mine.astype(F32) + other.astype(F32)
        parts = [pair[0]]
        for d, route in zip((2, 1, 3), exchange_routes(ranks, 2, True, (2, 1, 3))):
            parts.append(lax.ppermute(pair[d], "head", route))
        attn_out = functools.reduce(jnp.add, parts).astype(BF16).reshape(steps, batch, HALF)
    return attn_out, new_keys, new_values


def solution(mesh):
    in_specs = (
        P(None, None, "seq"),
        P("seq", "head"),
        P("seq", "head"),
        P("seq", "head"),
        P("head", "seq"),
        P(None, "seq", "head"),
        P(None, "seq", "head"),
        P(),
    )
    out_specs = (P(None, None, ("seq", "head")), P(None, None, "head"), P(None, None, "head"))
    return jax.shard_map(local, mesh=mesh, in_specs=in_specs, out_specs=out_specs, check_vma=False)
```

time: 60.1 us -> 48 us (0.80)
  blocking collectives: 0 us -> 11.5 us
  waiting for transfers between devices: 18.5 us -> 9.81 us
  local copies, waits for them, and re-layouts: 8.19 us -> 0.02 us
  Pallas kernels: 9.08 us -> 6.7 us
  other arithmetic: 2.88 us -> 0.6 us
  starting transfers between devices: 20.3 us -> 18.1 us
    all_to_all x2 -> x0, waiting for transfers between devices: 14.8 us -> none  [gather_all(): return lax.all_to_all(x, axis, 0, 0, tiled=True)]
    all_to_all x2 -> x0, starting transfers between devices: 12 us -> none  [gather_all(): return lax.all_to_all(x, axis, 0, 0, tiled=True)]
    all_to_all x0 -> x1, blocking collectives: none -> 11.5 us  [gather_all(): return lax.all_to_all(x, axis, 0, 0, tiled=True)]
    ppermute x3 -> x9, starting transfers between devices: 3.77 us -> 12.6 us  [the longest x3 4.52 us: local(): lax.ppermute(partial_sums, 'seq', route)]
    unnamed x8 -> x6, local copies, waits for them, and re-layouts: 7.42 us -> 0.01 us
    ppermute x3 -> x9, waiting for transfers between devices: 2.95 us -> 8.98 us  [the longest x3 3.1 us: local(): sums = [sums] + [lax.ppermute(sums, 'seq', route) for route in along_z]]
    pallas_call x1, Pallas kernels: 5.76 us -> 4.33 us  [local(): pl.pallas_call(functools.partial(attend_kernel, steps, heads, 2048, devic...]
    add x2 -> x1, other arithmetic: 1.33 us -> 0.01 us  [local(): pair = mine.astype(F32) + other.astype(F32)]
  transfers between devices with their start and end apart: 6 -> 10, of which waited for: 5 -> 7; matrix products, arithmetic and copies ran while one was open for 3% -> 0% of each run, Pallas kernels for 0% -> 0%
where the time goes in v2:
time: 48 us; the launch traced here: 47.5 us
  starting transfers between devices  18.1 us (38%)
  blocking collectives  11.5 us (24%)
  waiting for transfers between devices  9.81 us (20%)
  Pallas kernels  6.7 us (14%)
  between operations  0.69 us (1%)
  other arithmetic  0.6 us (1%)
    all_to_all x1, blocking collectives, gather_all(): return lax.all_to_all(x, axis, 0, 0, tiled=True)  11.5 us
    ppermute x1, starting transfers between devices, local(): other = lax.ppermute(other, 'head', [(i, i ^ 1) for i in range(2 * ranks)])  5.52 us
    ppermute x3, starting transfers between devices, local(): lax.ppermute(partial_sums, 'seq', route)  4.52 us
    ppermute x3, starting transfers between devices, local(): sums = [sums] + [lax.ppermute(sums, 'seq', route) for route in along_z]  4.42 us
    pallas_call x1, Pallas kernels, local(): pl.pallas_call(functools.partial(attend_kernel, steps, heads, 2048, devic...  4.33 us
    ppermute x3, starting transfers between devices, local(): parts.append(lax.ppermute(pair[d], 'head', route))  3.69 us
    ppermute x3, waiting for transfers between devices, local(): sums = [sums] + [lax.ppermute(sums, 'seq', route) for route in along_z]  3.1 us
    ppermute x3, waiting for transfers between devices, local(): lax.ppermute(partial_sums, 'seq', route)  2.98 us
  transfers between devices with their start and end apart: 10, of which 7 were waited for; matrix products, arithmetic and copies ran while one was open for 0% of the time, Pallas kernels for 0%

profile of v2, /device:TPU:1, one launch (start us, length us, event | category | flops | bytes accessed | tf_op | source)
XLA Modules:
  0.0 47.5 jit_solution(12563909076793076045)
XLA Ops:
  0.6 0.0 copy-start.1
  0.6 0.0 copy-start
  0.7 1.8 %projections.1 = (bf16[8,1280]{1,0:T(8,128)(2,1)S(1)}, f32[24,128]{1,0:T(8,128)S(1)}) custom-call(f32[3,128]{1,0:T(4,128)} %constant.2.clone.constants_hbm, s32[4]{0:T(128)} %lengths_hbm.1, bf16[2,4,512]{2,1,0:T(4,128)(2,1)} %hidden_hbm.1, bf16[512,128]{1,0:T(8,128)(2,1)} %wk_hbm.1, bf16[512,128]{1,0:T(8,128)(2,1)} %wv_hbm.1, bf16[512,1024]{1,0:T(8,128)(2,1)} %wq_hbm.1, ...), custom_call_target="tpu_custom_call" | custom-call | tf_op jit(solution)/shard_map/projections/pallas_call | solution.py:272
  2.5 3.7 %collective-permute-start.2 = (bf16[8,1280]{1,0:T(8,128)(2,1)S(1)}, bf16[8,1280]{1,0:T(8,128)(2,1)S(1)}, u32[]{:S(2)}, u32[]{:S(2)}) collective-permute-start(bf16[8,1280]{1,0:T(8,128)(2,1)S(1)} %get-tuple-element.11), channel_id=1, source_target_pairs={{0,16},{32,48},{64,80},{96,112},{8,24},{40,56},{72,88},{104,120},{... | collective-permute-start | bytes 61448 | tf_op jit(solution)/shard_map/sum_over_width/ppermute | solution.py:293
  6.2 0.9 %collective-permute-start.1 = (bf16[8,1280]{1,0:T(8,128)(2,1)S(1)}, bf16[8,1280]{1,0:T(8,128)(2,1)S(1)}, u32[]{:S(2)}, u32[]{:S(2)}) collective-permute-start(bf16[8,1280]{1,0:T(8,128)(2,1)S(1)} %get-tuple-element.11), channel_id=1, source_target_pairs={{0,24},{32,56},{64,88},{96,120},{8,16},{40,48},{72,80},{104,112},{... | collective-permute-start | bytes 61448 | tf_op jit(solution)/shard_map/sum_over_width/ppermute | solution.py:293
  7.0 0.0 collective-permute-start
  7.0 0.3 collective-permute-done.2
  7.3 2.7 %collective-permute-done.1 = bf16[8,1280]{1,0:T(8,128)(2,1)S(1)} collective-permute-done((bf16[8,1280]{1,0:T(8,128)(2,1)S(1)}, bf16[8,1280]{1,0:T(8,128)(2,1)S(1)}, u32[]{:S(2)}, u32[]{:S(2)}) %collective-permute-start.1) | collective-permute-done | bytes 20512 | tf_op jit(solution)/shard_map/sum_over_width/ppermute | solution.py:293
  10.0 0.0 collective-permute-done
  10.0 3.7 %collective-permute-start.5 = (bf16[8,1280]{1,0:T(8,128)(2,1)S(1)}, bf16[8,1280]{1,0:T(8,128)(2,1)S(1)}, u32[]{:S(2)}, u32[]{:S(2)}) collective-permute-start(bf16[8,1280]{1,0:T(8,128)(2,1)S(1)} %add_convert_fusion.sum0_ref), channel_id=1, source_target_pairs={{0,64},{8,72},{16,80},{24,88},{32,96},{40,104},{48,112},{56,120},{... | collective-permute-start | bytes 61448 | tf_op jit(solution)/shard_map/sum_over_width/ppermute | solution.py:295
  13.7 0.4 collective-permute-start.4
  14.1 0.3 collective-permute-start.3
  14.4 0.4 collective-permute-done.5.sum3_ref
  14.9 2.7 %collective-permute-done.4.sum2_ref = bf16[8,1280]{1,0:T(8,128)(2,1)S(1)} collective-permute-done((bf16[8,1280]{1,0:T(8,128)(2,1)S(1)}, bf16[8,1280]{1,0:T(8,128)(2,1)S(1)}, u32[]{:S(2)}, u32[]{:S(2)}) %collective-permute-start.4) | collective-permute-done | bytes 20512 | tf_op jit(solution)/shard_map/sum_over_width/ppermute | solution.py:295
  17.5 0.0 collective-permute-done.3.sum1_ref
  17.5 0.0 copy-done.1
  17.5 0.0 copy-done
  17.6 0.0 copy-start.2
  17.6 4.3 %attention.1 = (bf16[16,8,1152]{2,1,0:T(8,128)(2,1)S(1)}, bf16[2,4,128]{2,1,0:T(4,128)(2,1)}, bf16[2,4,128]{2,1,0:T(4,128)(2,1)}) custom-call(f32[24,128]{1,0:T(8,128)S(1)} %get-tuple-element.10.tables_ref, bf16[8,1280]{1,0:T(8,128)(2,1)S(1)} %add_convert_fusion.sum0_ref, bf16[8,1280]{1,0:T(8,128)(2,1)S(1)} %collective-permute-done.3.sum1_ref, ...), custom_call_target="tpu_custom_call" | custom-call | tf_op jit(solution)/shard_map/attention/pallas_call | solution.py:297
  21.9 11.5 %all_to_all.5.message_ref = bf16[16,8,1152]{2,1,0:T(8,128)(2,1)S(1)} all-to-all(bf16[16,8,1152]{2,1,0:T(8,128)(2,1)S(1)} %get-tuple-element.12), channel_id=1, replica_groups=mesh['seq'=16,'head'=8] {'seq'}, dimensions={0} | all-to-all | bytes 589824 | tf_op jit(solution)/shard_map/combine/all_to_all | solution.py:255
  33.4 0.0 copy-done.2
  33.4 0.5 %combine.1 = (bf16[4,8,64]{2,1,0:T(8,128)(2,1)S(1)}, bf16[4,8,64]{2,1,0:T(8,128)(2,1)S(1)}) custom-call(bf16[16,8,1152]{2,1,0:T(8,128)(2,1)S(1)} %all_to_all.5.message_ref, bf16[1024,512]{1,0:T(8,128)(2,1)S(1)} %copy-done.2), custom_call_target="tpu_custom_call" | custom-call | tf_op jit(solution)/shard_map/combine/pallas_call | solution.py:322
  34.0 5.5 %collective-permute-start.6 = (bf16[4,8,64]{2,1,0:T(8,128)(2,1)S(1)}, bf16[4,8,64]{2,1,0:T(8,128)(2,1)S(1)}, u32[]{:S(2)}, u32[]{:S(2)}) collective-permute-start(bf16[4,8,64]{2,1,0:T(8,128)(2,1)S(1)} %get-tuple-element.14), channel_id=1, source_target_pairs={{0,1},{1,0},{2,3},{3,2},{4,5},{5,4},{6,7},{7,6},{8,9},{9,8},{10,11... | collective-permute-start | bytes 12296 | tf_op jit(solution)/shard_map/sum_over_heads/ppermute | solution.py:330
  39.5 0.8 %collective-permute-done.6 = bf16[4,8,64]{2,1,0:T(8,128)(2,1)S(1)} collective-permute-done((bf16[4,8,64]{2,1,0:T(8,128)(2,1)S(1)}, bf16[4,8,64]{2,1,0:T(8,128)(2,1)S(1)}, u32[]{:S(2)}, u32[]{:S(2)}) %collective-permute-start.6) | collective-permute-done | bytes 4128 | tf_op jit(solution)/shard_map/sum_over_heads/ppermute | solution.py:330
  40.3 2.9 %collective-permute-start.7 = (f32[8,64]{1,0:T(8,128)S(1)}, f32[8,64]{1,0:T(8,128)S(1)}, u32[]{:S(2)}, u32[]{:S(2)}) collective-permute-start(f32[8,64]{1,0:T(8,128)S(1)} %get-tuple-element.17), channel_id=1, source_target_pairs={{0,4},{1,5},{2,6},{3,7},{4,0},{5,1},{6,2},{7,3},{8,12},{9,13},{10,... | collective-permute-start | bytes 6152 | tf_op jit(solution)/shard_map/sum_over_heads/ppermute | solution.py:334
  43.2 0.8 %collective-permute-start.9 = (f32[8,64]{1,0:T(8,128)S(1)}, f32[8,64]{1,0:T(8,128)S(1)}, u32[]{:S(2)}, u32[]{:S(2)}) collective-permute-start(f32[8,64]{1,0:T(8,128)S(1)} %get-tuple-element.18), channel_id=1, source_target_pairs={{0,6},{1,7},{2,4},{3,5},{4,2},{5,3},{6,0},{7,1},{8,14},{9,15},{10,... | collective-permute-start | bytes 6152 | tf_op jit(solution)/shard_map/sum_over_heads/ppermute | solution.py:334
  44.0 0.0 collective-permute-start.8
  44.0 0.3 collective-permute-done.7
  44.3 2.6 %collective-permute-done.9 = f32[8,64]{1,0:T(8,128)S(1)} collective-permute-done((f32[8,64]{1,0:T(8,128)S(1)}, f32[8,64]{1,0:T(8,128)S(1)}, u32[]{:S(2)}, u32[]{:S(2)}) %collective-permute-start.9) | collective-permute-done | bytes 2080 | tf_op jit(solution)/shard_map/sum_over_heads/ppermute | solution.py:334
  46.9 0.0 collective-permute-done.8
  46.9 0.6 %fusion.3 = bf16[8,64]{1,0:T(8,128)(2,1)} fusion(f32[8,64]{1,0:T(8,128)S(1)} %collective-permute-done.9, f32[8,64]{1,0:T(8,128)S(1)} %collective-permute-done.8, f32[8,64]{1,0:T(8,128)S(1)} %collective-permute-done.7, f32[4,8,64]{2,1,0:T(8,128)S(1)} %convert_add_fusion), kind=kLoop, calls=%fused_computation.9 | loop fusion | flops 2048 | bytes 9216 | tf_op jit(solution)/shard_map/sum_over_heads/convert_element_type | solution.py:335
  (3 shorter events, 0.0 us)
Async XLA Ops:
  0.6 16.9 %copy-start.1 = (bf16[4,8192,128]{2,1,0:T(8,128)(2,1)S(1)}, bf16[4,8192,128]{2,1,0:T(8,128)(2,1)}, u32[]{:S(2)}) copy-start(bf16[4,8192,128]{2,1,0:T(8,128)(2,1)} %refs_1_.1) | copy-start | bytes 25165828
  0.6 16.9 %copy-start = (bf16[4,8192,128]{2,1,0:T(8,128)(2,1)S(1)}, bf16[4,8192,128]{2,1,0:T(8,128)(2,1)}, u32[]{:S(2)}) copy-start(bf16[4,8192,128]{2,1,0:T(8,128)(2,1)} %refs_0_.1) | copy-start | bytes 25165828
  2.5 4.8 %collective-permute-start.2 = (bf16[8,1280]{1,0:T(8,128)(2,1)S(1)}, bf16[8,1280]{1,0:T(8,128)(2,1)S(1)}, u32[]{:S(2)}, u32[]{:S(2)}) collective-permute-start(bf16[8,1280]{1,0:T(8,128)(2,1)S(1)} %get-tuple-element.11), channel_id=1, source_target_pairs={{0,16},{32,48},{64,80},{96,112},{8,24},{40,56},{72,88},{104,120},{... | collective-permute-start | bytes 61448 | tf_op jit(solution)/shard_map/sum_over_width/ppermute | solution.py:293
  6.2 3.8 %collective-permute-start.1 = (bf16[8,1280]{1,0:T(8,128)(2,1)S(1)}, bf16[8,1280]{1,0:T(8,128)(2,1)S(1)}, u32[]{:S(2)}, u32[]{:S(2)}) collective-permute-start(bf16[8,1280]{1,0:T(8,128)(2,1)S(1)} %get-tuple-element.11), channel_id=1, source_target_pairs={{0,24},{32,56},{64,88},{96,120},{8,16},{40,48},{72,80},{104,112},{... | collective-permute-start | bytes 61448 | tf_op jit(solution)/shard_map/sum_over_width/ppermute | solution.py:293
  7.0 3.0 %collective-permute-start = (bf16[8,1280]{1,0:T(8,128)(2,1)S(1)}, bf16[8,1280]{1,0:T(8,128)(2,1)S(1)}, u32[]{:S(2)}, u32[]{:S(2)}) collective-permute-start(bf16[8,1280]{1,0:T(8,128)(2,1)S(1)} %get-tuple-element.11), channel_id=1, source_target_pairs={{0,8},{32,40},{64,72},{96,104},{8,0},{40,32},{72,64},{104,96},{16,... | collective-permute-start | bytes 61448 | tf_op jit(solution)/shard_map/sum_over_width/ppermute | solution.py:293
  10.0 4.8 %collective-permute-start.5 = (bf16[8,1280]{1,0:T(8,128)(2,1)S(1)}, bf16[8,1280]{1,0:T(8,128)(2,1)S(1)}, u32[]{:S(2)}, u32[]{:S(2)}) collective-permute-start(bf16[8,1280]{1,0:T(8,128)(2,1)S(1)} %add_convert_fusion.sum0_ref), channel_id=1, source_target_pairs={{0,64},{8,72},{16,80},{24,88},{32,96},{40,104},{48,112},{56,120},{... | collective-permute-start | bytes 61448 | tf_op jit(solution)/shard_map/sum_over_width/ppermute | solution.py:295
  13.7 3.8 %collective-permute-start.4 = (bf16[8,1280]{1,0:T(8,128)(2,1)S(1)}, bf16[8,1280]{1,0:T(8,128)(2,1)S(1)}, u32[]{:S(2)}, u32[]{:S(2)}) collective-permute-start(bf16[8,1280]{1,0:T(8,128)(2,1)S(1)} %add_convert_fusion.sum0_ref), channel_id=1, source_target_pairs={{0,96},{8,104},{16,112},{24,120},{32,64},{40,72},{48,80},{56,88},{... | collective-permute-start | bytes 61448 | tf_op jit(solution)/shard_map/sum_over_width/ppermute | solution.py:295
  14.1 3.4 %collective-permute-start.3 = (bf16[8,1280]{1,0:T(8,128)(2,1)S(1)}, bf16[8,1280]{1,0:T(8,128)(2,1)S(1)}, u32[]{:S(2)}, u32[]{:S(2)}) collective-permute-start(bf16[8,1280]{1,0:T(8,128)(2,1)S(1)} %add_convert_fusion.sum0_ref), channel_id=1, source_target_pairs={{0,32},{8,40},{16,48},{24,56},{32,0},{40,8},{48,16},{56,24},{64,96... | collective-permute-start | bytes 61448 | tf_op jit(solution)/shard_map/sum_over_width/ppermute | solution.py:295
  17.6 15.9 %copy-start.2 = (bf16[1024,512]{1,0:T(8,128)(2,1)S(1)}, bf16[1024,512]{1,0:T(8,128)(2,1)}, u32[]{:S(2)}) copy-start(bf16[1024,512]{1,0:T(8,128)(2,1)} %w_out_ref.1) | copy-start | bytes 3145732
  34.0 6.3 %collective-permute-start.6 = (bf16[4,8,64]{2,1,0:T(8,128)(2,1)S(1)}, bf16[4,8,64]{2,1,0:T(8,128)(2,1)S(1)}, u32[]{:S(2)}, u32[]{:S(2)}) collective-permute-start(bf16[4,8,64]{2,1,0:T(8,128)(2,1)S(1)} %get-tuple-element.14), channel_id=1, source_target_pairs={{0,1},{1,0},{2,3},{3,2},{4,5},{5,4},{6,7},{7,6},{8,9},{9,8},{10,11... | collective-permute-start | bytes 12296 | tf_op jit(solution)/shard_map/sum_over_heads/ppermute | solution.py:330
  40.3 4.0 %collective-permute-start.7 = (f32[8,64]{1,0:T(8,128)S(1)}, f32[8,64]{1,0:T(8,128)S(1)}, u32[]{:S(2)}, u32[]{:S(2)}) collective-permute-start(f32[8,64]{1,0:T(8,128)S(1)} %get-tuple-element.17), channel_id=1, source_target_pairs={{0,4},{1,5},{2,6},{3,7},{4,0},{5,1},{6,2},{7,3},{8,12},{9,13},{10,... | collective-permute-start | bytes 6152 | tf_op jit(solution)/shard_map/sum_over_heads/ppermute | solution.py:334
  43.2 3.7 %collective-permute-start.9 = (f32[8,64]{1,0:T(8,128)S(1)}, f32[8,64]{1,0:T(8,128)S(1)}, u32[]{:S(2)}, u32[]{:S(2)}) collective-permute-start(f32[8,64]{1,0:T(8,128)S(1)} %get-tuple-element.18), channel_id=1, source_target_pairs={{0,6},{1,7},{2,4},{3,5},{4,2},{5,3},{6,0},{7,1},{8,14},{9,15},{10,... | collective-permute-start | bytes 6152 | tf_op jit(solution)/shard_map/sum_over_heads/ppermute | solution.py:334
  44.0 2.9 %collective-permute-start.8 = (f32[8,64]{1,0:T(8,128)S(1)}, f32[8,64]{1,0:T(8,128)S(1)}, u32[]{:S(2)}, u32[]{:S(2)}) collective-permute-start(f32[8,64]{1,0:T(8,128)S(1)} %get-tuple-element.19), channel_id=1, source_target_pairs={{0,2},{1,3},{2,0},{3,1},{4,6},{5,7},{6,4},{7,5},{8,10},{9,11},{10,... | collective-permute-start | bytes 6152 | tf_op jit(solution)/shard_map/sum_over_heads/ppermute | solution.py:334

commit v3 on v2

--- a/solution.py
+++ b/solution.py
@@ -64,13 +64,14 @@
     kv_width = wk_ref.shape[1]
     copies[3].wait()
     key = jnp.dot(hidden, wk_ref[...], preferred_element_type=F32)
-    out_ref[:, q_width : q_width + kv_width] = key.astype(BF16)
     copies[4].wait()
     value = jnp.dot(hidden, wv_ref[...], preferred_element_type=F32)
-    out_ref[:, q_width + kv_width :] = value.astype(BF16)
     copies[5].wait()
     query = jnp.dot(hidden, wq_ref[...], preferred_element_type=F32)
-    out_ref[:, :q_width] = query.astype(BF16)
+    for c in range(out_ref.shape[0]):
+        out_ref[c, :, :q_width] = query.astype(BF16)
+        out_ref[c, :, q_width : q_width + kv_width] = key.astype(BF16)
+        out_ref[c, :, q_width + kv_width :] = value.astype(BF16)
 
 
 def fetch_kernel(first, source_ref, target_ref, sem):
@@ -85,7 +86,7 @@
 
 
 def attend_kernel(
-    steps, heads, chunk, copies, tables_ref, sum0_ref, sum1_ref, sum2_ref, sum3_ref, *refs
+    steps, heads, chunk, copies, tables_ref, sums_ref, *refs
 ):
     *keys_refs, values_ref, message_ref, new_keys_hbm, new_values_hbm = refs[:-8]
     query_scr, scores_scr, out_scr, value_buf, new_keys_ref, new_values_ref, value_sems, new_sems = refs[-8:]
@@ -97,9 +98,9 @@
 
     rows = steps * batch
     group = steps * heads
-    total = sum0_ref[...].astype(F32)
-    for part_ref in (sum1_ref, sum2_ref, sum3_ref):
-        total = total + part_ref[...].astype(F32)
+    total = sums_ref[0].astype(F32)
+    for d in range(1, sums_ref.shape[0]):
+        total = total + sums_ref[d].astype(F32)
     cosine = tables_ref[:rows]
     sine = tables_ref[rows : 2 * rows]
 
@@ -272,7 +273,7 @@
         partial_sums, tables = pl.pallas_call(
             functools.partial(project_kernel, steps),
             out_shape=(
-                jax.ShapeDtypeStruct((rows, (heads + 2) * width), BF16),
+                jax.ShapeDtypeStruct((devices, rows, (heads + 2) * width), BF16),
                 jax.ShapeDtypeStruct((3 * rows, width), F32),
             ),
             in_specs=[anywhere] * 8,
@@ -288,11 +289,7 @@
         )(x)
 
     with jax.named_scope("sum_over_width"):
-        along_x = exchange_routes(4, devices // 4, False)
-        along_z = exchange_routes(4, devices // 4, True)
-        sums = [partial_sums] + [lax.ppermute(partial_sums, "seq", route) for route in along_x]
-        sums = functools.reduce(jnp.add, [x.astype(F32) for x in sums]).astype(BF16)
-        sums = [sums] + [lax.ppermute(sums, "seq", route) for route in along_z]
+        sums = gather_all(partial_sums, "seq")
     with jax.named_scope("attention"):
         message, new_keys, new_values = pl.pallas_call(
             functools.partial(attend_kernel, steps, heads, 2048, devices),
@@ -301,7 +298,7 @@
                 jax.ShapeDtypeStruct((steps, batch, width), BF16),
                 jax.ShapeDtypeStruct((steps, batch, width), BF16),
             ),
-            in_specs=[whole] * 7,
+            in_specs=[whole] * 4,
             out_specs=(whole, anywhere, anywhere),
             scratch_shapes=[
                 pltpu.VMEM((batch, steps * heads, width), F32),
@@ -314,7 +311,7 @@
                 pltpu.SemaphoreType.DMA((2,)),
             ],
             compiler_params=pltpu.CompilerParams(vmem_limit_bytes=16 * 2**20),
-        )(tables, *sums, in_vmem(key_cache), in_vmem(value_cache))
+        )(tables, sums, in_vmem(key_cache), in_vmem(value_cache))
     with jax.named_scope("combine"):
         messages = gather_all(message, "seq")
         ranks = lax.axis_size("head") // 2

time: 48 us -> 46.5 us (0.969)
  blocking collectives: 11.5 us -> 27.3 us
  starting transfers between devices: 18.1 us -> 6.97 us
  waiting for transfers between devices: 9.81 us -> 3.72 us
    all_to_all x1 -> x2, blocking collectives: 11.5 us -> 27.3 us  [gather_all(): return lax.all_to_all(x, axis, 0, 0, tiled=True)]
    ppermute x6 -> x0, starting transfers between devices: 8.93 us -> none  [the longest x3 4.52 us: local(): lax.ppermute(partial_sums, 'seq', route)]
    ppermute x6 -> x0, waiting for transfers between devices: 6.09 us -> none  [the longest x3 3.1 us: local(): sums = [sums] + [lax.ppermute(sums, 'seq', route) for route in along_z]]
    ppermute x1, starting transfers between devices: 5.52 us -> 3.28 us  [local(): other = lax.ppermute(other, 'head', [(i, i ^ 1) for i in range(2 * ranks)])]
  transfers between devices with their start and end apart: 10 -> 4, of which waited for: 7 -> 3; matrix products, arithmetic and copies ran while one was open for 0% -> 0% of each run, Pallas kernels for 0% -> 0%
where the time goes in v3:
time: 46.5 us; the launch traced here: 46 us
  blocking collectives  27.3 us (59%)
  starting transfers between devices  6.97 us (15%)
  Pallas kernels  6.74 us (14%)
  waiting for transfers between devices  3.72 us (8%)
  between operations  0.67 us (1%)
  other arithmetic  0.59 us (1%)
    all_to_all x2, blocking collectives, gather_all(): return lax.all_to_all(x, axis, 0, 0, tiled=True)  27.3 us
    pallas_call x1, Pallas kernels, local(): pl.pallas_call(functools.partial(attend_kernel, steps, heads, 2048, devic...  4.37 us
    ppermute x3, starting transfers between devices, local(): parts.append(lax.ppermute(pair[d], 'head', route))  3.69 us
    ppermute x1, starting transfers between devices, local(): other = lax.ppermute(other, 'head', [(i, i ^ 1) for i in range(2 * ranks)])  3.28 us
    ppermute x3, waiting for transfers between devices, local(): parts.append(lax.ppermute(pair[d], 'head', route))  2.89 us
    pallas_call x1, Pallas kernels, local(): pl.pallas_call(functools.partial(project_kernel, steps), out_shape=(jax.S...  1.85 us
  transfers between devices with their start and end apart: 4, of which 3 were waited for; matrix products, arithmetic and copies ran while one was open for 0% of the time, Pallas kernels for 0%

profile of v3, /device:TPU:1, one launch (start us, length us, event | category | flops | bytes accessed | tf_op | source)
XLA Modules:
  0.0 46.0 jit_solution(329667111780762650)
XLA Ops:
  0.6 0.0 copy-start.1
  0.6 0.0 copy-start
  0.7 1.9 %projections.1 = (bf16[16,8,1280]{2,1,0:T(8,128)(2,1)S(1)}, f32[24,128]{1,0:T(8,128)S(1)}) custom-call(f32[3,128]{1,0:T(4,128)} %constant.2.clone.constants_hbm, s32[4]{0:T(128)} %lengths_hbm.1, bf16[2,4,512]{2,1,0:T(4,128)(2,1)} %hidden_hbm.1, bf16[512,128]{1,0:T(8,128)(2,1)} %wk_hbm.1, bf16[512,128]{1,0:T(8,128)(2,1)} %wv_hbm.1, bf16[512,1024]{1,0:T(8,128)(2,1)} %wq_hbm.1, ...), custom_call_target="tpu_custom_call" | custom-call | tf_op jit(solution)/shard_map/projections/pallas_call | solution.py:273
  2.5 17.0 %all_to_all.10.sums_ref = bf16[16,8,1280]{2,1,0:T(8,128)(2,1)S(1)} all-to-all(bf16[16,8,1280]{2,1,0:T(8,128)(2,1)S(1)} %get-tuple-element.11), channel_id=1, replica_groups=mesh['seq'=16,'head'=8] {'seq'}, dimensions={0} | all-to-all | bytes 655360 | tf_op jit(solution)/shard_map/sum_over_width/all_to_all | solution.py:256
  19.5 0.0 copy-done.1
  19.5 0.0 copy-done
  19.5 0.0 copy-start.2
  19.5 4.4 %attention.1 = (bf16[16,8,1152]{2,1,0:T(8,128)(2,1)S(1)}, bf16[2,4,128]{2,1,0:T(4,128)(2,1)}, bf16[2,4,128]{2,1,0:T(4,128)(2,1)}) custom-call(f32[24,128]{1,0:T(8,128)S(1)} %get-tuple-element.10.tables_ref, bf16[16,8,1280]{2,1,0:T(8,128)(2,1)S(1)} %all_to_all.10.sums_ref, bf16[4,8192,128]{2,1,0:T(8,128)(2,1)S(1)} %copy-done, bf16[4,8192,128]{2,1,0:T(8,128)(2,1)S(1)} %copy-done.1), custom_call_target="tpu_custom_call" | custom-call | tf_op jit(solution)/shard_map/attention/pallas_call | solution.py:294
  23.9 10.3 %all_to_all.11.message_ref = bf16[16,8,1152]{2,1,0:T(8,128)(2,1)S(1)} all-to-all(bf16[16,8,1152]{2,1,0:T(8,128)(2,1)S(1)} %get-tuple-element.12), channel_id=1, replica_groups=mesh['seq'=16,'head'=8] {'seq'}, dimensions={0} | all-to-all | bytes 589824 | tf_op jit(solution)/shard_map/combine/all_to_all | solution.py:256
  34.2 0.0 copy-done.2
  34.2 0.5 %combine.1 = (bf16[4,8,64]{2,1,0:T(8,128)(2,1)S(1)}, bf16[4,8,64]{2,1,0:T(8,128)(2,1)S(1)}) custom-call(bf16[16,8,1152]{2,1,0:T(8,128)(2,1)S(1)} %all_to_all.11.message_ref, bf16[1024,512]{1,0:T(8,128)(2,1)S(1)} %copy-done.2), custom_call_target="tpu_custom_call" | custom-call | tf_op jit(solution)/shard_map/combine/pallas_call | solution.py:319
  34.7 3.3 %collective-permute-start = (bf16[4,8,64]{2,1,0:T(8,128)(2,1)S(1)}, bf16[4,8,64]{2,1,0:T(8,128)(2,1)S(1)}, u32[]{:S(2)}, u32[]{:S(2)}) collective-permute-start(bf16[4,8,64]{2,1,0:T(8,128)(2,1)S(1)} %get-tuple-element.14), channel_id=1, source_target_pairs={{0,1},{1,0},{2,3},{3,2},{4,5},{5,4},{6,7},{7,6},{8,9},{9,8},{10,11... | collective-permute-start | bytes 12296 | tf_op jit(solution)/shard_map/sum_over_heads/ppermute | solution.py:327
  38.0 0.8 %collective-permute-done = bf16[4,8,64]{2,1,0:T(8,128)(2,1)S(1)} collective-permute-done((bf16[4,8,64]{2,1,0:T(8,128)(2,1)S(1)}, bf16[4,8,64]{2,1,0:T(8,128)(2,1)S(1)}, u32[]{:S(2)}, u32[]{:S(2)}) %collective-permute-start) | collective-permute-done | bytes 4128 | tf_op jit(solution)/shard_map/sum_over_heads/ppermute | solution.py:327
  38.8 2.9 %collective-permute-start.1 = (f32[8,64]{1,0:T(8,128)S(1)}, f32[8,64]{1,0:T(8,128)S(1)}, u32[]{:S(2)}, u32[]{:S(2)}) collective-permute-start(f32[8,64]{1,0:T(8,128)S(1)} %get-tuple-element.17), channel_id=1, source_target_pairs={{0,4},{1,5},{2,6},{3,7},{4,0},{5,1},{6,2},{7,3},{8,12},{9,13},{10,... | collective-permute-start | bytes 6152 | tf_op jit(solution)/shard_map/sum_over_heads/ppermute | solution.py:331
  41.7 0.8 %collective-permute-start.3 = (f32[8,64]{1,0:T(8,128)S(1)}, f32[8,64]{1,0:T(8,128)S(1)}, u32[]{:S(2)}, u32[]{:S(2)}) collective-permute-start(f32[8,64]{1,0:T(8,128)S(1)} %get-tuple-element.18), channel_id=1, source_target_pairs={{0,6},{1,7},{2,4},{3,5},{4,2},{5,3},{6,0},{7,1},{8,14},{9,15},{10,... | collective-permute-start | bytes 6152 | tf_op jit(solution)/shard_map/sum_over_heads/ppermute | solution.py:331
  42.5 0.0 collective-permute-start.2
  42.5 0.3 collective-permute-done.1
  42.8 2.6 %collective-permute-done.3 = f32[8,64]{1,0:T(8,128)S(1)} collective-permute-done((f32[8,64]{1,0:T(8,128)S(1)}, f32[8,64]{1,0:T(8,128)S(1)}, u32[]{:S(2)}, u32[]{:S(2)}) %collective-permute-start.3) | collective-permute-done | bytes 2080 | tf_op jit(solution)/shard_map/sum_over_heads/ppermute | solution.py:331
  45.4 0.0 collective-permute-done.2
  45.4 0.6 %fusion.3 = bf16[8,64]{1,0:T(8,128)(2,1)} fusion(f32[8,64]{1,0:T(8,128)S(1)} %collective-permute-done.3, f32[8,64]{1,0:T(8,128)S(1)} %collective-permute-done.2, f32[8,64]{1,0:T(8,128)S(1)} %collective-permute-done.1, f32[4,8,64]{2,1,0:T(8,128)S(1)} %convert_add_fusion), kind=kLoop, calls=%fused_computation.8 | loop fusion | flops 2048 | bytes 9216 | tf_op jit(solution)/shard_map/sum_over_heads/convert_element_type | solution.py:332
  (2 shorter events, 0.0 us)
Async XLA Ops:
  0.6 18.8 %copy-start.1 = (bf16[4,8192,128]{2,1,0:T(8,128)(2,1)S(1)}, bf16[4,8192,128]{2,1,0:T(8,128)(2,1)}, u32[]{:S(2)}) copy-start(bf16[4,8192,128]{2,1,0:T(8,128)(2,1)} %refs_1_.1) | copy-start | bytes 25165828
  0.6 18.8 %copy-start = (bf16[4,8192,128]{2,1,0:T(8,128)(2,1)S(1)}, bf16[4,8192,128]{2,1,0:T(8,128)(2,1)}, u32[]{:S(2)}) copy-start(bf16[4,8192,128]{2,1,0:T(8,128)(2,1)} %refs_0_.1) | copy-start | bytes 25165828
  19.5 14.7 %copy-start.2 = (bf16[1024,512]{1,0:T(8,128)(2,1)S(1)}, bf16[1024,512]{1,0:T(8,128)(2,1)}, u32[]{:S(2)}) copy-start(bf16[1024,512]{1,0:T(8,128)(2,1)} %w_out_ref.1) | copy-start | bytes 3145732
  34.7 4.1 %collective-permute-start = (bf16[4,8,64]{2,1,0:T(8,128)(2,1)S(1)}, bf16[4,8,64]{2,1,0:T(8,128)(2,1)S(1)}, u32[]{:S(2)}, u32[]{:S(2)}) collective-permute-start(bf16[4,8,64]{2,1,0:T(8,128)(2,1)S(1)} %get-tuple-element.14), channel_id=1, source_target_pairs={{0,1},{1,0},{2,3},{3,2},{4,5},{5,4},{6,7},{7,6},{8,9},{9,8},{10,11... | collective-permute-start | bytes 12296 | tf_op jit(solution)/shard_map/sum_over_heads/ppermute | solution.py:327
  38.8 4.0 %collective-permute-start.1 = (f32[8,64]{1,0:T(8,128)S(1)}, f32[8,64]{1,0:T(8,128)S(1)}, u32[]{:S(2)}, u32[]{:S(2)}) collective-permute-start(f32[8,64]{1,0:T(8,128)S(1)} %get-tuple-element.17), channel_id=1, source_target_pairs={{0,4},{1,5},{2,6},{3,7},{4,0},{5,1},{6,2},{7,3},{8,12},{9,13},{10,... | collective-permute-start | bytes 6152 | tf_op jit(solution)/shard_map/sum_over_heads/ppermute | solution.py:331
  41.7 3.7 %collective-permute-start.3 = (f32[8,64]{1,0:T(8,128)S(1)}, f32[8,64]{1,0:T(8,128)S(1)}, u32[]{:S(2)}, u32[]{:S(2)}) collective-permute-start(f32[8,64]{1,0:T(8,128)S(1)} %get-tuple-element.18), channel_id=1, source_target_pairs={{0,6},{1,7},{2,4},{3,5},{4,2},{5,3},{6,0},{7,1},{8,14},{9,15},{10,... | collective-permute-start | bytes 6152 | tf_op jit(solution)/shard_map/sum_over_heads/ppermute | solution.py:331
  42.5 2.9 %collective-permute-start.2 = (f32[8,64]{1,0:T(8,128)S(1)}, f32[8,64]{1,0:T(8,128)S(1)}, u32[]{:S(2)}, u32[]{:S(2)}) collective-permute-start(f32[8,64]{1,0:T(8,128)S(1)} %get-tuple-element.19), channel_id=1, source_target_pairs={{0,2},{1,3},{2,0},{3,1},{4,6},{5,7},{6,4},{7,5},{8,10},{9,11},{10,... | collective-permute-start | bytes 6152 | tf_op jit(solution)/shard_map/sum_over_heads/ppermute | solution.py:331

commit v4 on v3

--- a/solution.py
+++ b/solution.py
@@ -27,12 +27,13 @@
     return np.concatenate([fine, coarse, sign]).astype(np.float32)
 
 
-def note_kernel(x_ref, o_ref):
-    o_ref[...] = x_ref[...]
+def announce_kernel(keys_ref, values_ref, tables_ref, out_ref):
+    del keys_ref, values_ref
+    out_ref[...] = tables_ref[...]
 
 
 def project_kernel(
-    steps, constants_hbm, lengths_hbm, hidden_hbm, wk_hbm, wv_hbm, wq_hbm, _, __, out_ref, tables_ref,
+    steps, constants_hbm, lengths_hbm, hidden_hbm, wk_hbm, wv_hbm, wq_hbm, out_ref, tables_ref,
     constants_ref, lengths_ref, hidden_ref, wk_ref, wv_ref, wq_ref, sems,
 ):
     pairs = [
@@ -74,28 +75,19 @@
         out_ref[c, :, q_width + kv_width :] = value.astype(BF16)
 
 
-def fetch_kernel(first, source_ref, target_ref, sem):
-    batch = target_ref.shape[0]
-    copies = [
-        pltpu.make_async_copy(source_ref.at[first + b], target_ref.at[b], sem.at[b]) for b in range(batch)
-    ]
-    for copy in copies:
-        copy.start()
-    for copy in copies:
-        copy.wait()
+def split(x, count):
+    parts = []
+    for _ in range(count):
+        parts.append(x.astype(BF16).astype(F32))
+        x = x - parts[-1]
+    return parts
 
 
 def attend_kernel(
-    steps, heads, chunk, copies, tables_ref, sums_ref, *refs
+    steps, heads, chunk, copies, tables_ref, sums_ref, keys_ref, values_ref, message_ref, new_keys_hbm, new_values_hbm,
+    query_scr, scores_scr, out_scr, new_keys_ref, new_values_ref, new_sems,
 ):
-    *keys_refs, values_ref, message_ref, new_keys_hbm, new_values_hbm = refs[:-8]
-    query_scr, scores_scr, out_scr, value_buf, new_keys_ref, new_values_ref, value_sems, new_sems = refs[-8:]
     batch, context, width = values_ref.shape
-    each = batch // len(keys_refs)
-
-    def fetch(b):
-        return pltpu.make_async_copy(values_ref.at[b], value_buf.at[b], value_sems.at[b])
-
     rows = steps * batch
     group = steps * heads
     total = sums_ref[0].astype(F32)
@@ -136,12 +128,11 @@
     tops = []
     for b in range(batch):
         query = query_scr[b].astype(BF16)
-        keys_ref = keys_refs[b // each]
         limit = tables_ref[2 * rows + b : 2 * rows + b + 1, :1].astype(jnp.int32) - first
         top = jnp.full((group, chunk), FILL, F32)
         for start in range(0, context, chunk):
             scores = lax.dot_general(
-                query, keys_ref[b % each, start : start + chunk, :], (((1,), (1,)), ((), ())),
+                query, keys_ref[b, start : start + chunk, :], (((1,), (1,)), ((), ())),
                 preferred_element_type=F32,
             )
             scores = jnp.where(position < limit - start, scores, FILL)
@@ -159,7 +150,6 @@
             fresh.append(jnp.where(row_step >= t, score, FILL))
         fresh_top = functools.reduce(jnp.maximum, fresh)
         top = jnp.where(owner, jnp.maximum(top, fresh_top), top)
-        top = top.astype(BF16).astype(F32)
         weight_sum = jnp.zeros((group, chunk), F32)
         out = jnp.zeros((group, width), F32)
         for start in range(0, context, chunk):
@@ -178,12 +168,10 @@
             weight = weight.astype(BF16).astype(F32) * fresh_scale
             weight_sum = weight_sum + weight
             out = out + weight * new_value[row : row + 1]
-        sum_high = weight_sum.astype(BF16).astype(F32)
-        sum_low = weight_sum - sum_high
-        stats = jnp.where(
-            stat_lane == 0, top,
-            jnp.where(stat_lane == heads, sum_high, jnp.where(stat_lane == 2 * heads, sum_low, 0.0)),
-        )
+        parts = split(top, 3) + split(weight_sum, 2)
+        stats = jnp.zeros((group, width), F32)
+        for i, part in enumerate(parts):
+            stats = jnp.where(stat_lane == i * heads, part, stats)
         for s in range(steps):
             r = s * batch + b
             out_scr[r : r + 1, heads * width :] = jnp.sum(
@@ -198,19 +186,22 @@
         copy.wait()
 
 
-def combine_kernel(heads, message_ref, w_out_ref, mine_ref, other_ref):
+def combine_kernel(heads, message_ref, w_out_ref, out_ref):
     devices, rows, _ = message_ref.shape
     width = HEAD_WIDTH
-    stats = [message_ref[d, :, heads * width :].astype(F32) for d in range(devices)]
-    top = functools.reduce(jnp.maximum, stats)
+    lane = lax.broadcasted_iota(jnp.int32, (rows, width), 1)
+    tops, sums = [], []
+    for d in range(devices):
+        stats = message_ref[d, :, heads * width :].astype(F32)
+        parts = [stats] + [pltpu.roll(stats, width - i * heads, 1) for i in range(1, 5)]
+        tops.append(jnp.where(lane < heads, (parts[0] + parts[1]) + parts[2], 0.0))
+        sums.append(parts[3] + parts[4])
+    top = functools.reduce(jnp.maximum, tops)
     total = jnp.zeros((rows, width), F32)
     factors = []
-    lane = lax.broadcasted_iota(jnp.int32, (rows, width), 1)
     for d in range(devices):
-        factor = jnp.exp(jnp.where(lane < heads, stats[d] - top, 0.0))
-        sums = pltpu.roll(stats[d], width - heads, 1) + pltpu.roll(stats[d], width - 2 * heads, 1)
-        total = total + factor * sums
-        factors.append(factor)
+        factors.append(jnp.exp(tops[d] - top))
+        total = total + factors[d] * sums[d]
     scale = 1.0 / jnp.where(lane < heads, total, 1.0)
     factors = [f * scale for f in factors]
     attended = []
@@ -224,28 +215,24 @@
     projected = jnp.dot(attended, w_out_ref[...], preferred_element_type=F32)
     head = lax.axis_index("head")
     rank = head // 2
-    first_core = head % 2 == 0
-    for target in range(mine_ref.shape[0]):
-        block = projected[:, target * width : (target + 1) * width]
-        swapped = pltpu.roll(block, HALF, 1)
+    for target in range(out_ref.shape[0]):
         slot = jnp.bitwise_xor(rank, target)
-        mine_ref[slot] = jnp.where(first_core, block, swapped)[:, :HALF].astype(BF16)
-        other_ref[slot] = jnp.where(first_core, swapped, block)[:, :HALF].astype(BF16)
+        out_ref[slot] = projected[:, target * width : (target + 1) * width].astype(BF16)
+
+
+def finish_kernel(pair_ref, part1_ref, part2_ref, part3_ref, out_ref):
+    total = pair_ref[0]
+    for part_ref in (part1_ref, part2_ref, part3_ref):
+        total = total + part_ref[...]
+    first_core = lax.axis_index("head") % 2 == 0
+    total = jnp.where(first_core, total, pltpu.roll(total, HALF, 1))[:, :HALF]
+    steps, batch, _ = out_ref.shape
+    for s in range(steps):
+        out_ref[s] = total[s * batch : (s + 1) * batch].astype(BF16)
 
 
 def in_vmem(x):
     return pltpu.with_memory_space_constraint(x, VMEM)
-
-
-def exchange_routes(count, inner, axis_inner, order=(1, 3, 2)):
-    routes = []
-    for d in order:
-        pairs = []
-        for i in range(count):
-            for j in range(inner):
-                pairs.append((i * inner + j, (i ^ d) * inner + j) if axis_inner else (j * count + i, j * count + (i ^ d)))
-        routes.append(pairs)
-    return routes
 
 
 def in_hbm(x):
@@ -267,28 +254,31 @@
 
     with jax.named_scope("projections"):
         operands = (jnp.asarray(rotary_tables()), lengths, hidden, key_matrix, value_matrix, w_query)
-        buffers = [
-            (pltpu.SMEM if x.ndim == 1 else pltpu.VMEM)(x.shape, x.dtype) for x in operands
-        ]
+        buffers = [(pltpu.SMEM if x.ndim == 1 else pltpu.VMEM)(x.shape, x.dtype) for x in operands]
         partial_sums, tables = pl.pallas_call(
             functools.partial(project_kernel, steps),
             out_shape=(
                 jax.ShapeDtypeStruct((devices, rows, (heads + 2) * width), BF16),
                 jax.ShapeDtypeStruct((3 * rows, width), F32),
             ),
-            in_specs=[anywhere] * 8,
+            in_specs=[anywhere] * 6,
             out_specs=(whole, whole),
             scratch_shapes=buffers + [pltpu.SemaphoreType.DMA((6,))],
             compiler_params=pltpu.CompilerParams(vmem_limit_bytes=4 * 2**20),
-        )(*[in_hbm(x) for x in operands], in_hbm(key_cache), in_hbm(value_cache))
-    def note(x):
+        )(*[in_hbm(x) for x in operands])
+
+    def announced(x):
         return pl.pallas_call(
-            note_kernel, out_shape=jax.ShapeDtypeStruct(x.shape, x.dtype), in_specs=[whole], out_specs=whole,
-            cost_estimate=pl.CostEstimate(flops=0, bytes_accessed=16800000, transcendentals=0),
+            announce_kernel,
+            out_shape=jax.ShapeDtypeStruct(x.shape, x.dtype),
+            in_specs=[anywhere, anywhere, whole],
+            out_specs=whole,
             compiler_params=pltpu.CompilerParams(vmem_limit_bytes=2**20),
-        )(x)
+        )(in_hbm(key_cache), in_hbm(value_cache), x)
 
     with jax.named_scope("sum_over_width"):
+        tables = announced(announced(announced(tables)))
+        partial_sums, tables = lax.optimization_barrier((partial_sums, tables))
         sums = gather_all(partial_sums, "seq")
     with jax.named_scope("attention"):
         message, new_keys, new_values = pl.pallas_call(
@@ -304,10 +294,8 @@
                 pltpu.VMEM((batch, steps * heads, width), F32),
                 pltpu.VMEM((batch, steps * heads, key_cache.shape[1]), F32),
                 pltpu.VMEM((rows, (heads + 1) * width), F32),
-                pltpu.VMEM((1,8,128), BF16),
                 pltpu.VMEM((steps, batch, width), BF16),
                 pltpu.VMEM((steps, batch, width), BF16),
-                pltpu.SemaphoreType.DMA((batch,)),
                 pltpu.SemaphoreType.DMA((2,)),
             ],
             compiler_params=pltpu.CompilerParams(vmem_limit_bytes=16 * 2**20),
@@ -315,21 +303,27 @@
     with jax.named_scope("combine"):
         messages = gather_all(message, "seq")
         ranks = lax.axis_size("head") // 2
-        part = jax.ShapeDtypeStruct((ranks, rows, HALF), BF16)
-        mine, other = pl.pallas_call(
+        projected = pl.pallas_call(
             functools.partial(combine_kernel, heads),
-            out_shape=(part, part),
+            out_shape=jax.ShapeDtypeStruct((ranks, rows, width), BF16),
             in_specs=[whole, whole],
-            out_specs=(whole, whole),
+            out_specs=whole,
             compiler_params=pltpu.CompilerParams(vmem_limit_bytes=4 * 2**20),
         )(in_vmem(messages), in_vmem(w_out))
     with jax.named_scope("sum_over_heads"):
-        other = lax.ppermute(other, "head", [(i, i ^ 1) for i in range(2 * ranks)])
-        pair = mine.astype(F32) + other.astype(F32)
-        parts = [pair[0]]
-        for d, route in zip((2, 1, 3), exchange_routes(ranks, 2, True, (2, 1, 3))):
+        other = lax.ppermute(projected, "head", [(i, i ^ 1) for i in range(2 * ranks)])
+        pair = projected.astype(F32) + other.astype(F32)
+        parts = []
+        for d, crossed in ((1, 0), (3, 0), (2, 1)):
+            route = [(2 * y + c, 2 * (y ^ d) + (c ^ crossed)) for y in range(ranks) for c in range(2)]
             parts.append(lax.ppermute(pair[d], "head", route))
-        attn_out = functools.reduce(jnp.add, parts).astype(BF16).reshape(steps, batch, HALF)
+        attn_out = pl.pallas_call(
+            finish_kernel,
+            out_shape=jax.ShapeDtypeStruct((steps, batch, HALF), BF16),
+            in_specs=[whole] * 4,
+            out_specs=whole,
+            compiler_params=pltpu.CompilerParams(vmem_limit_bytes=2**20),
+        )(pair, *parts)
     return attn_out, new_keys, new_values
 
 

time: 46.5 us -> 46.3 us (level)
  other arithmetic: 0.59 us -> 0.01 us
    pallas_call x1 -> x5, Pallas kernels: 0.53 us -> 1.13 us  [the longest x1 0.65 us: local(): pl.pallas_call(finish_kernel, out_shape=jax.ShapeDtypeStruct((steps, batc...]
    convert_element_type x1 -> x0, other arithmetic: 0.58 us -> none  [local(): functools.reduce(jnp.add, parts).astype(BF16).reshape(steps, batch, HALF)]
where the time goes in v4:
time: 46.3 us; the launch traced here: 46.2 us
  blocking collectives  27.3 us (59%)
  starting transfers between devices  7.2 us (16%)
  Pallas kernels  7.17 us (15%)
  waiting for transfers between devices  3.72 us (8%)
  between operations  0.75 us (2%)
    all_to_all x2, blocking collectives, gather_all(): return lax.all_to_all(x, axis, 0, 0, tiled=True)  27.3 us
    pallas_call x1, Pallas kernels, local(): pl.pallas_call(functools.partial(attend_kernel, steps, heads, 2048, devic...  4.33 us
    ppermute x3, starting transfers between devices, local(): parts.append(lax.ppermute(pair[d], 'head', route))  3.92 us
    ppermute x1, starting transfers between devices, local(): lax.ppermute(projected, 'head', [(i, i ^ 1) for i in range(2 * ranks)])  3.28 us
    ppermute x3, waiting for transfers between devices, local(): parts.append(lax.ppermute(pair[d], 'head', route))  2.89 us
    pallas_call x1, Pallas kernels, local(): pl.pallas_call(functools.partial(project_kernel, steps), out_shape=(jax.S...  1.71 us
  transfers between devices with their start and end apart: 4, of which 3 were waited for; matrix products, arithmetic and copies ran while one was open for 0% of the time, Pallas kernels for 0%

profile of v4, /device:TPU:1, one launch (start us, length us, event | category | flops | bytes accessed | tf_op | source)
XLA Modules:
  0.0 46.2 jit_solution(12447020177997282507)
XLA Ops:
  0.6 1.7 %projections.1 = (bf16[16,8,1280]{2,1,0:T(8,128)(2,1)S(1)}, f32[24,128]{1,0:T(8,128)S(1)}) custom-call(f32[3,128]{1,0:T(4,128)} %constant.2.clone.constants_hbm, s32[4]{0:T(128)} %lengths_hbm.1, bf16[2,4,512]{2,1,0:T(4,128)(2,1)} %hidden_hbm.1, bf16[512,128]{1,0:T(8,128)(2,1)} %wk_hbm.1, bf16[512,128]{1,0:T(8,128)(2,1)} %wv_hbm.1, bf16[512,1024]{1,0:T(8,128)(2,1)} %wq_hbm.1), custom_call_target="tpu_custom_call" | custom-call | tf_op jit(solution)/shard_map/projections/pallas_call | solution.py:258
  2.4 0.0 slice-start
  2.4 0.0 slice-start.2
  2.4 0.0 slice-start.1
  2.4 0.0 slice-start.3
  2.4 17.0 %all_to_all.10.sums_ref = bf16[16,8,1280]{2,1,0:T(8,128)(2,1)S(1)} all-to-all(bf16[16,8,1280]{2,1,0:T(8,128)(2,1)S(1)} %get-tuple-element.13), channel_id=1, replica_groups=mesh['seq'=16,'head'=8] {'seq'}, dimensions={0} | all-to-all | bytes 655360 | tf_op jit(solution)/shard_map/sum_over_width/all_to_all | solution.py:243
  19.4 0.0 slice-done
  19.4 0.0 slice-done.2
  19.4 0.0 slice-done.1
  19.4 0.0 slice-done.3
  19.4 0.0 copy-start
  19.5 4.3 %attention.1 = (bf16[16,8,1152]{2,1,0:T(8,128)(2,1)S(1)}, bf16[2,4,128]{2,1,0:T(4,128)(2,1)}, bf16[2,4,128]{2,1,0:T(4,128)(2,1)}) custom-call(f32[24,128]{1,0:T(8,128)S(1)} %sum_over_width.5.tables_ref, bf16[16,8,1280]{2,1,0:T(8,128)(2,1)S(1)} %all_to_all.10.sums_ref, bf16[4,8192,128]{2,1,0:T(8,128)(2,1)S(1)} %bitcast.7, bf16[4,8192,128]{2,1,0:T(8,128)(2,1)S(1)} %bitcast.9), custom_call_target="tpu_custom_call" | custom-call | tf_op jit(solution)/shard_map/attention/pallas_call | solution.py:284
  23.8 10.3 %all_to_all.11.message_ref = bf16[16,8,1152]{2,1,0:T(8,128)(2,1)S(1)} all-to-all(bf16[16,8,1152]{2,1,0:T(8,128)(2,1)S(1)} %get-tuple-element.14), channel_id=1, replica_groups=mesh['seq'=16,'head'=8] {'seq'}, dimensions={0} | all-to-all | bytes 589824 | tf_op jit(solution)/shard_map/combine/all_to_all | solution.py:243
  34.1 0.0 copy-done
  34.1 0.5 %combine.1 = bf16[4,8,128]{2,1,0:T(8,128)(2,1)S(1)} custom-call(bf16[16,8,1152]{2,1,0:T(8,128)(2,1)S(1)} %all_to_all.11.message_ref, bf16[1024,512]{1,0:T(8,128)(2,1)S(1)} %copy-done), custom_call_target="tpu_custom_call" | custom-call | tf_op jit(solution)/shard_map/combine/pallas_call | solution.py:306
  34.6 3.3 %collective-permute-start = (bf16[4,8,128]{2,1,0:T(8,128)(2,1)S(1)}, bf16[4,8,128]{2,1,0:T(8,128)(2,1)S(1)}, u32[]{:S(2)}, u32[]{:S(2)}) collective-permute-start(bf16[4,8,128]{2,1,0:T(8,128)(2,1)S(1)} %combine.1), channel_id=1, source_target_pairs={{0,1},{1,0},{2,3},{3,2},{4,5},{5,4},{6,7},{7,6},{8,9},{9,8},{10,11... | collective-permute-start | bytes 24584 | tf_op jit(solution)/shard_map/sum_over_heads/ppermute | solution.py:314
  37.9 0.8 %collective-permute-done = bf16[4,8,128]{2,1,0:T(8,128)(2,1)S(1)} collective-permute-done((bf16[4,8,128]{2,1,0:T(8,128)(2,1)S(1)}, bf16[4,8,128]{2,1,0:T(8,128)(2,1)S(1)}, u32[]{:S(2)}, u32[]{:S(2)}) %collective-permute-start) | collective-permute-done | bytes 8224 | tf_op jit(solution)/shard_map/sum_over_heads/ppermute | solution.py:314
  38.7 3.1 %collective-permute-start.3 = (f32[8,128]{1,0:T(8,128)S(1)}, f32[8,128]{1,0:T(8,128)S(1)}, u32[]{:S(2)}, u32[]{:S(2)}) collective-permute-start(f32[8,128]{1,0:T(8,128)S(1)} %get-tuple-element.17), channel_id=1, source_target_pairs={{0,5},{1,4},{2,7},{3,6},{4,1},{5,0},{6,3},{7,2},{8,13},{9,12},{10,... | collective-permute-start | bytes 12296 | tf_op jit(solution)/shard_map/sum_over_heads/ppermute | solution.py:319
  41.8 0.8 %collective-permute-start.2 = (f32[8,128]{1,0:T(8,128)S(1)}, f32[8,128]{1,0:T(8,128)S(1)}, u32[]{:S(2)}, u32[]{:S(2)}) collective-permute-start(f32[8,128]{1,0:T(8,128)S(1)} %get-tuple-element.18), channel_id=1, source_target_pairs={{0,6},{1,7},{2,4},{3,5},{4,2},{5,3},{6,0},{7,1},{8,14},{9,15},{10,... | collective-permute-start | bytes 12296 | tf_op jit(solution)/shard_map/sum_over_heads/ppermute | solution.py:319
  42.6 0.0 collective-permute-start.1
  42.6 0.6 %collective-permute-done.3.part3_ref = f32[8,128]{1,0:T(8,128)S(1)} collective-permute-done((f32[8,128]{1,0:T(8,128)S(1)}, f32[8,128]{1,0:T(8,128)S(1)}, u32[]{:S(2)}, u32[]{:S(2)}) %collective-permute-start.3) | collective-permute-done | bytes 4128 | tf_op jit(solution)/shard_map/sum_over_heads/ppermute | solution.py:319
  43.2 2.3 %collective-permute-done.2.part2_ref = f32[8,128]{1,0:T(8,128)S(1)} collective-permute-done((f32[8,128]{1,0:T(8,128)S(1)}, f32[8,128]{1,0:T(8,128)S(1)}, u32[]{:S(2)}, u32[]{:S(2)}) %collective-permute-start.2) | collective-permute-done | bytes 4128 | tf_op jit(solution)/shard_map/sum_over_heads/ppermute | solution.py:319
  45.5 0.0 collective-permute-done.1.part1_ref
  45.5 0.7 %sum_over_heads.1 = bf16[2,4,64]{2,1,0:T(4,128)(2,1)} custom-call(f32[4,8,128]{2,1,0:T(8,128)S(1)} %convert_add_fusion.pair_ref, f32[8,128]{1,0:T(8,128)S(1)} %collective-permute-done.1.part1_ref, f32[8,128]{1,0:T(8,128)S(1)} %collective-permute-done.2.part2_ref, f32[8,128]{1,0:T(8,128)S(1)} %collective-permute-done.3.part3_ref), custom_call_target="tpu_custom_call" | custom-call | tf_op jit(solution)/shard_map/sum_over_heads/pallas_call | solution.py:320
  (7 shorter events, 0.0 us)
Async XLA Ops:
  2.4 17.0 %slice-start = ((s8[8388608]{0:T(1024)(128)(4,1)}), s8[4194304]{0:T(1024)(128)(4,1)S(1)}, s32[]{:S(2)}) async-start(s8[8388608]{0:T(1024)(128)(4,1)} %bitcast.6), calls=%async_computation.2 | async-start | bytes 8388608
  2.4 17.0 %slice-start.2 = ((s8[8388608]{0:T(1024)(128)(4,1)}), s8[4194304]{0:T(1024)(128)(4,1)S(1)}, s32[]{:S(2)}) async-start(s8[8388608]{0:T(1024)(128)(4,1)} %bitcast.8), calls=%async_computation.4 | async-start | bytes 8388608
  2.4 17.0 %slice-start.1 = ((s8[8388608]{0:T(1024)(128)(4,1)}), s8[4194304]{0:T(1024)(128)(4,1)S(1)}, s32[]{:S(2)}) async-start(s8[8388608]{0:T(1024)(128)(4,1)} %bitcast.6), calls=%async_computation.3 | async-start | bytes 8388608
  2.4 17.0 %slice-start.3 = ((s8[8388608]{0:T(1024)(128)(4,1)}), s8[4194304]{0:T(1024)(128)(4,1)S(1)}, s32[]{:S(2)}) async-start(s8[8388608]{0:T(1024)(128)(4,1)} %bitcast.8), calls=%async_computation.5 | async-start | bytes 8388608
  19.4 14.7 %copy-start = (bf16[1024,512]{1,0:T(8,128)(2,1)S(1)}, bf16[1024,512]{1,0:T(8,128)(2,1)}, u32[]{:S(2)}) copy-start(bf16[1024,512]{1,0:T(8,128)(2,1)} %w_out_ref.1) | copy-start | bytes 3145732
  34.6 4.1 %collective-permute-start = (bf16[4,8,128]{2,1,0:T(8,128)(2,1)S(1)}, bf16[4,8,128]{2,1,0:T(8,128)(2,1)S(1)}, u32[]{:S(2)}, u32[]{:S(2)}) collective-permute-start(bf16[4,8,128]{2,1,0:T(8,128)(2,1)S(1)} %combine.1), channel_id=1, source_target_pairs={{0,1},{1,0},{2,3},{3,2},{4,5},{5,4},{6,7},{7,6},{8,9},{9,8},{10,11... | collective-permute-start | bytes 24584 | tf_op jit(solution)/shard_map/sum_over_heads/ppermute | solution.py:314
  38.7 4.5 %collective-permute-start.3 = (f32[8,128]{1,0:T(8,128)S(1)}, f32[8,128]{1,0:T(8,128)S(1)}, u32[]{:S(2)}, u32[]{:S(2)}) collective-permute-start(f32[8,128]{1,0:T(8,128)S(1)} %get-tuple-element.17), channel_id=1, source_target_pairs={{0,5},{1,4},{2,7},{3,6},{4,1},{5,0},{6,3},{7,2},{8,13},{9,12},{10,... | collective-permute-start | bytes 12296 | tf_op jit(solution)/shard_map/sum_over_heads/ppermute | solution.py:319
  41.8 3.7 %collective-permute-start.2 = (f32[8,128]{1,0:T(8,128)S(1)}, f32[8,128]{1,0:T(8,128)S(1)}, u32[]{:S(2)}, u32[]{:S(2)}) collective-permute-start(f32[8,128]{1,0:T(8,128)S(1)} %get-tuple-element.18), channel_id=1, source_target_pairs={{0,6},{1,7},{2,4},{3,5},{4,2},{5,3},{6,0},{7,1},{8,14},{9,15},{10,... | collective-permute-start | bytes 12296 | tf_op jit(solution)/shard_map/sum_over_heads/ppermute | solution.py:319
  42.6 2.9 %collective-permute-start.1 = (f32[8,128]{1,0:T(8,128)S(1)}, f32[8,128]{1,0:T(8,128)S(1)}, u32[]{:S(2)}, u32[]{:S(2)}) collective-permute-start(f32[8,128]{1,0:T(8,128)S(1)} %get-tuple-element.19), channel_id=1, source_target_pairs={{0,2},{1,3},{2,0},{3,1},{4,6},{5,7},{6,4},{7,5},{8,10},{9,11},{10,... | collective-permute-start | bytes 12296 | tf_op jit(solution)/shard_map/sum_over_heads/ppermute | solution.py:319

commit v5 on v4

--- a/solution.py
+++ b/solution.py
@@ -204,15 +204,19 @@
         total = total + factors[d] * sums[d]
     scale = 1.0 / jnp.where(lane < heads, total, 1.0)
     factors = [f * scale for f in factors]
-    attended = []
-    for h in range(heads):
-        mixed = jnp.zeros((rows, width), F32)
-        for d in range(devices):
-            part = message_ref[d, :, h * width : (h + 1) * width].astype(F32)
-            mixed = mixed + factors[d][:, h : h + 1] * part
-        attended.append(mixed.astype(BF16))
-    attended = jnp.concatenate(attended, axis=1)
-    projected = jnp.dot(attended, w_out_ref[...], preferred_element_type=F32)
+    projected = jnp.zeros((rows, w_out_ref.shape[1]), F32)
+    for first in range(0, heads, 2):
+        attended = []
+        for h in range(first, first + 2):
+            mixed = jnp.zeros((rows, width), F32)
+            for d in range(devices):
+                part = message_ref[d, :, h * width : (h + 1) * width].astype(F32)
+                mixed = mixed + factors[d][:, h : h + 1] * part
+            attended.append(mixed.astype(BF16))
+        rows_of_w = w_out_ref[first * width : (first + 2) * width, :]
+        projected = projected + jnp.dot(
+            jnp.concatenate(attended, axis=1), rows_of_w, preferred_element_type=F32
+        )
     head = lax.axis_index("head")
     rank = head // 2
     for target in range(out_ref.shape[0]):

time: 46.3 us -> 46.4 us (level)
  no operation moved by 1% of the time
where the time goes in v5:
time: 46.4 us; the launch traced here: 46.2 us
  blocking collectives  27.3 us (59%)
  starting transfers between devices  7.2 us (16%)
  Pallas kernels  7.19 us (15%)
  waiting for transfers between devices  3.72 us (8%)
  between operations  0.75 us (2%)
    all_to_all x2, blocking collectives, gather_all(): return lax.all_to_all(x, axis, 0, 0, tiled=True)  27.3 us
    pallas_call x1, Pallas kernels, local(): pl.pallas_call(functools.partial(attend_kernel, steps, heads, 2048, devic...  4.33 us
    ppermute x3, starting transfers between devices, local(): parts.append(lax.ppermute(pair[d], 'head', route))  3.92 us
    ppermute x1, starting transfers between devices, local(): lax.ppermute(projected, 'head', [(i, i ^ 1) for i in range(2 * ranks)])  3.28 us
    ppermute x3, waiting for transfers between devices, local(): parts.append(lax.ppermute(pair[d], 'head', route))  2.89 us
    pallas_call x1, Pallas kernels, local(): pl.pallas_call(functools.partial(project_kernel, steps), out_shape=(jax.S...  1.71 us
  transfers between devices with their start and end apart: 4, of which 3 were waited for; matrix products, arithmetic and copies ran while one was open for 0% of the time, Pallas kernels for 0%

profile of v5, /device:TPU:1, one launch (start us, length us, event | category | flops | bytes accessed | tf_op | source)
XLA Modules:
  0.0 46.2 jit_solution(2463145900793415805)
XLA Ops:
  0.6 1.7 %projections.1 = (bf16[16,8,1280]{2,1,0:T(8,128)(2,1)S(1)}, f32[24,128]{1,0:T(8,128)S(1)}) custom-call(f32[3,128]{1,0:T(4,128)} %constant.2.clone.constants_hbm, s32[4]{0:T(128)} %lengths_hbm.1, bf16[2,4,512]{2,1,0:T(4,128)(2,1)} %hidden_hbm.1, bf16[512,128]{1,0:T(8,128)(2,1)} %wk_hbm.1, bf16[512,128]{1,0:T(8,128)(2,1)} %wv_hbm.1, bf16[512,1024]{1,0:T(8,128)(2,1)} %wq_hbm.1), custom_call_target="tpu_custom_call" | custom-call | tf_op jit(solution)/shard_map/projections/pallas_call | solution.py:262
  2.4 0.0 slice-start
  2.4 0.0 slice-start.2
  2.4 0.0 slice-start.1
  2.4 0.0 slice-start.3
  2.4 17.0 %all_to_all.10.sums_ref = bf16[16,8,1280]{2,1,0:T(8,128)(2,1)S(1)} all-to-all(bf16[16,8,1280]{2,1,0:T(8,128)(2,1)S(1)} %get-tuple-element.13), channel_id=1, replica_groups=mesh['seq'=16,'head'=8] {'seq'}, dimensions={0} | all-to-all | bytes 655360 | tf_op jit(solution)/shard_map/sum_over_width/all_to_all | solution.py:247
  19.4 0.0 slice-done
  19.4 0.0 slice-done.2
  19.4 0.0 slice-done.1
  19.4 0.0 slice-done.3
  19.4 0.0 copy-start
  19.5 4.3 %attention.1 = (bf16[16,8,1152]{2,1,0:T(8,128)(2,1)S(1)}, bf16[2,4,128]{2,1,0:T(4,128)(2,1)}, bf16[2,4,128]{2,1,0:T(4,128)(2,1)}) custom-call(f32[24,128]{1,0:T(8,128)S(1)} %sum_over_width.5.tables_ref, bf16[16,8,1280]{2,1,0:T(8,128)(2,1)S(1)} %all_to_all.10.sums_ref, bf16[4,8192,128]{2,1,0:T(8,128)(2,1)S(1)} %bitcast.7, bf16[4,8192,128]{2,1,0:T(8,128)(2,1)S(1)} %bitcast.9), custom_call_target="tpu_custom_call" | custom-call | tf_op jit(solution)/shard_map/attention/pallas_call | solution.py:288
  23.8 10.3 %all_to_all.11.message_ref = bf16[16,8,1152]{2,1,0:T(8,128)(2,1)S(1)} all-to-all(bf16[16,8,1152]{2,1,0:T(8,128)(2,1)S(1)} %get-tuple-element.14), channel_id=1, replica_groups=mesh['seq'=16,'head'=8] {'seq'}, dimensions={0} | all-to-all | bytes 589824 | tf_op jit(solution)/shard_map/combine/all_to_all | solution.py:247
  34.1 0.0 copy-done
  34.1 0.5 %combine.1 = bf16[4,8,128]{2,1,0:T(8,128)(2,1)S(1)} custom-call(bf16[16,8,1152]{2,1,0:T(8,128)(2,1)S(1)} %all_to_all.11.message_ref, bf16[1024,512]{1,0:T(8,128)(2,1)S(1)} %copy-done), custom_call_target="tpu_custom_call" | custom-call | tf_op jit(solution)/shard_map/combine/pallas_call | solution.py:310
  34.6 3.3 %collective-permute-start = (bf16[4,8,128]{2,1,0:T(8,128)(2,1)S(1)}, bf16[4,8,128]{2,1,0:T(8,128)(2,1)S(1)}, u32[]{:S(2)}, u32[]{:S(2)}) collective-permute-start(bf16[4,8,128]{2,1,0:T(8,128)(2,1)S(1)} %combine.1), channel_id=1, source_target_pairs={{0,1},{1,0},{2,3},{3,2},{4,5},{5,4},{6,7},{7,6},{8,9},{9,8},{10,11... | collective-permute-start | bytes 24584 | tf_op jit(solution)/shard_map/sum_over_heads/ppermute | solution.py:318
  37.9 0.8 %collective-permute-done = bf16[4,8,128]{2,1,0:T(8,128)(2,1)S(1)} collective-permute-done((bf16[4,8,128]{2,1,0:T(8,128)(2,1)S(1)}, bf16[4,8,128]{2,1,0:T(8,128)(2,1)S(1)}, u32[]{:S(2)}, u32[]{:S(2)}) %collective-permute-start) | collective-permute-done | bytes 8224 | tf_op jit(solution)/shard_map/sum_over_heads/ppermute | solution.py:318
  38.7 3.1 %collective-permute-start.3 = (f32[8,128]{1,0:T(8,128)S(1)}, f32[8,128]{1,0:T(8,128)S(1)}, u32[]{:S(2)}, u32[]{:S(2)}) collective-permute-start(f32[8,128]{1,0:T(8,128)S(1)} %get-tuple-element.17), channel_id=1, source_target_pairs={{0,5},{1,4},{2,7},{3,6},{4,1},{5,0},{6,3},{7,2},{8,13},{9,12},{10,... | collective-permute-start | bytes 12296 | tf_op jit(solution)/shard_map/sum_over_heads/ppermute | solution.py:323
  41.9 0.8 %collective-permute-start.2 = (f32[8,128]{1,0:T(8,128)S(1)}, f32[8,128]{1,0:T(8,128)S(1)}, u32[]{:S(2)}, u32[]{:S(2)}) collective-permute-start(f32[8,128]{1,0:T(8,128)S(1)} %get-tuple-element.18), channel_id=1, source_target_pairs={{0,6},{1,7},{2,4},{3,5},{4,2},{5,3},{6,0},{7,1},{8,14},{9,15},{10,... | collective-permute-start | bytes 12296 | tf_op jit(solution)/shard_map/sum_over_heads/ppermute | solution.py:323
  42.6 0.0 collective-permute-start.1
  42.6 0.6 %collective-permute-done.3.part3_ref = f32[8,128]{1,0:T(8,128)S(1)} collective-permute-done((f32[8,128]{1,0:T(8,128)S(1)}, f32[8,128]{1,0:T(8,128)S(1)}, u32[]{:S(2)}, u32[]{:S(2)}) %collective-permute-start.3) | collective-permute-done | bytes 4128 | tf_op jit(solution)/shard_map/sum_over_heads/ppermute | solution.py:323
  43.3 2.3 %collective-permute-done.2.part2_ref = f32[8,128]{1,0:T(8,128)S(1)} collective-permute-done((f32[8,128]{1,0:T(8,128)S(1)}, f32[8,128]{1,0:T(8,128)S(1)}, u32[]{:S(2)}, u32[]{:S(2)}) %collective-permute-start.2) | collective-permute-done | bytes 4128 | tf_op jit(solution)/shard_map/sum_over_heads/ppermute | solution.py:323
  45.5 0.0 collective-permute-done.1.part1_ref
  45.5 0.7 %sum_over_heads.1 = bf16[2,4,64]{2,1,0:T(4,128)(2,1)} custom-call(f32[4,8,128]{2,1,0:T(8,128)S(1)} %convert_add_fusion.pair_ref, f32[8,128]{1,0:T(8,128)S(1)} %collective-permute-done.1.part1_ref, f32[8,128]{1,0:T(8,128)S(1)} %collective-permute-done.2.part2_ref, f32[8,128]{1,0:T(8,128)S(1)} %collective-permute-done.3.part3_ref), custom_call_target="tpu_custom_call" | custom-call | tf_op jit(solution)/shard_map/sum_over_heads/pallas_call | solution.py:324
  (7 shorter events, 0.0 us)
Async XLA Ops:
  2.4 17.0 %slice-start = ((s8[8388608]{0:T(1024)(128)(4,1)}), s8[4194304]{0:T(1024)(128)(4,1)S(1)}, s32[]{:S(2)}) async-start(s8[8388608]{0:T(1024)(128)(4,1)} %bitcast.6), calls=%async_computation.2 | async-start | bytes 8388608
  2.4 17.0 %slice-start.2 = ((s8[8388608]{0:T(1024)(128)(4,1)}), s8[4194304]{0:T(1024)(128)(4,1)S(1)}, s32[]{:S(2)}) async-start(s8[8388608]{0:T(1024)(128)(4,1)} %bitcast.8), calls=%async_computation.4 | async-start | bytes 8388608
  2.4 17.0 %slice-start.1 = ((s8[8388608]{0:T(1024)(128)(4,1)}), s8[4194304]{0:T(1024)(128)(4,1)S(1)}, s32[]{:S(2)}) async-start(s8[8388608]{0:T(1024)(128)(4,1)} %bitcast.6), calls=%async_computation.3 | async-start | bytes 8388608
  2.4 17.0 %slice-start.3 = ((s8[8388608]{0:T(1024)(128)(4,1)}), s8[4194304]{0:T(1024)(128)(4,1)S(1)}, s32[]{:S(2)}) async-start(s8[8388608]{0:T(1024)(128)(4,1)} %bitcast.8), calls=%async_computation.5 | async-start | bytes 8388608
  19.4 14.7 %copy-start = (bf16[1024,512]{1,0:T(8,128)(2,1)S(1)}, bf16[1024,512]{1,0:T(8,128)(2,1)}, u32[]{:S(2)}) copy-start(bf16[1024,512]{1,0:T(8,128)(2,1)} %w_out_ref.1) | copy-start | bytes 3145732
  34.6 4.1 %collective-permute-start = (bf16[4,8,128]{2,1,0:T(8,128)(2,1)S(1)}, bf16[4,8,128]{2,1,0:T(8,128)(2,1)S(1)}, u32[]{:S(2)}, u32[]{:S(2)}) collective-permute-start(bf16[4,8,128]{2,1,0:T(8,128)(2,1)S(1)} %combine.1), channel_id=1, source_target_pairs={{0,1},{1,0},{2,3},{3,2},{4,5},{5,4},{6,7},{7,6},{8,9},{9,8},{10,11... | collective-permute-start | bytes 24584 | tf_op jit(solution)/shard_map/sum_over_heads/ppermute | solution.py:318
  38.7 4.5 %collective-permute-start.3 = (f32[8,128]{1,0:T(8,128)S(1)}, f32[8,128]{1,0:T(8,128)S(1)}, u32[]{:S(2)}, u32[]{:S(2)}) collective-permute-start(f32[8,128]{1,0:T(8,128)S(1)} %get-tuple-element.17), channel_id=1, source_target_pairs={{0,5},{1,4},{2,7},{3,6},{4,1},{5,0},{6,3},{7,2},{8,13},{9,12},{10,... | collective-permute-start | bytes 12296 | tf_op jit(solution)/shard_map/sum_over_heads/ppermute | solution.py:323
  41.9 3.7 %collective-permute-start.2 = (f32[8,128]{1,0:T(8,128)S(1)}, f32[8,128]{1,0:T(8,128)S(1)}, u32[]{:S(2)}, u32[]{:S(2)}) collective-permute-start(f32[8,128]{1,0:T(8,128)S(1)} %get-tuple-element.18), channel_id=1, source_target_pairs={{0,6},{1,7},{2,4},{3,5},{4,2},{5,3},{6,0},{7,1},{8,14},{9,15},{10,... | collective-permute-start | bytes 12296 | tf_op jit(solution)/shard_map/sum_over_heads/ppermute | solution.py:323
  42.6 2.9 %collective-permute-start.1 = (f32[8,128]{1,0:T(8,128)S(1)}, f32[8,128]{1,0:T(8,128)S(1)}, u32[]{:S(2)}, u32[]{:S(2)}) collective-permute-start(f32[8,128]{1,0:T(8,128)S(1)} %get-tuple-element.19), channel_id=1, source_target_pairs={{0,2},{1,3},{2,0},{3,1},{4,6},{5,7},{6,4},{7,5},{8,10},{9,11},{10,... | collective-permute-start | bytes 12296 | tf_op jit(solution)/shard_map/sum_over_heads/ppermute | solution.py:323

commit v6 on v4

--- a/solution.py
+++ b/solution.py
@@ -282,7 +282,7 @@
         sums = gather_all(partial_sums, "seq")
     with jax.named_scope("attention"):
         message, new_keys, new_values = pl.pallas_call(
-            functools.partial(attend_kernel, steps, heads, 2048, devices),
+            functools.partial(attend_kernel, steps, heads, key_cache.shape[1], devices),
             out_shape=(
                 jax.ShapeDtypeStruct((devices, rows, (heads + 1) * width), BF16),
                 jax.ShapeDtypeStruct((steps, batch, width), BF16),

time: 46.3 us -> 46.3 us (level)
  no operation moved by 1% of the time
where the time goes in v6:
time: 46.3 us; the launch traced here: 46.1 us
  blocking collectives  27.3 us (59%)
  starting transfers between devices  7.2 us (16%)
  Pallas kernels  7.11 us (15%)
  waiting for transfers between devices  3.72 us (8%)
  between operations  0.75 us (2%)
    all_to_all x2, blocking collectives, gather_all(): return lax.all_to_all(x, axis, 0, 0, tiled=True)  27.3 us
    pallas_call x1, Pallas kernels, local(): pl.pallas_call(functools.partial(attend_kernel, steps, heads, key_cache.s...  4.27 us
    ppermute x3, starting transfers between devices, local(): parts.append(lax.ppermute(pair[d], 'head', route))  3.92 us
    ppermute x1, starting transfers between devices, local(): lax.ppermute(projected, 'head', [(i, i ^ 1) for i in range(2 * ranks)])  3.28 us
    ppermute x3, waiting for transfers between devices, local(): parts.append(lax.ppermute(pair[d], 'head', route))  2.89 us
    pallas_call x1, Pallas kernels, local(): pl.pallas_call(functools.partial(project_kernel, steps), out_shape=(jax.S...  1.71 us
  transfers between devices with their start and end apart: 4, of which 3 were waited for; matrix products, arithmetic and copies ran while one was open for 0% of the time, Pallas kernels for 0%

profile of v6, /device:TPU:1, one launch (start us, length us, event | category | flops | bytes accessed | tf_op | source)
XLA Modules:
  0.0 46.1 jit_solution(12779740663153062747)
XLA Ops:
  0.6 1.7 %projections.1 = (bf16[16,8,1280]{2,1,0:T(8,128)(2,1)S(1)}, f32[24,128]{1,0:T(8,128)S(1)}) custom-call(f32[3,128]{1,0:T(4,128)} %constant.2.clone.constants_hbm, s32[4]{0:T(128)} %lengths_hbm.1, bf16[2,4,512]{2,1,0:T(4,128)(2,1)} %hidden_hbm.1, bf16[512,128]{1,0:T(8,128)(2,1)} %wk_hbm.1, bf16[512,128]{1,0:T(8,128)(2,1)} %wv_hbm.1, bf16[512,1024]{1,0:T(8,128)(2,1)} %wq_hbm.1), custom_call_target="tpu_custom_call" | custom-call | tf_op jit(solution)/shard_map/projections/pallas_call | solution.py:258
  2.4 0.0 slice-start
  2.4 0.0 slice-start.2
  2.4 0.0 slice-start.1
  2.4 0.0 slice-start.3
  2.4 17.0 %all_to_all.10.sums_ref = bf16[16,8,1280]{2,1,0:T(8,128)(2,1)S(1)} all-to-all(bf16[16,8,1280]{2,1,0:T(8,128)(2,1)S(1)} %get-tuple-element.13), channel_id=1, replica_groups=mesh['seq'=16,'head'=8] {'seq'}, dimensions={0} | all-to-all | bytes 655360 | tf_op jit(solution)/shard_map/sum_over_width/all_to_all | solution.py:243
  19.4 0.0 slice-done
  19.4 0.0 slice-done.2
  19.4 0.0 slice-done.1
  19.4 0.0 slice-done.3
  19.4 0.0 copy-start
  19.5 4.3 %attention.1 = (bf16[16,8,1152]{2,1,0:T(8,128)(2,1)S(1)}, bf16[2,4,128]{2,1,0:T(4,128)(2,1)}, bf16[2,4,128]{2,1,0:T(4,128)(2,1)}) custom-call(f32[24,128]{1,0:T(8,128)S(1)} %sum_over_width.5.tables_ref, bf16[16,8,1280]{2,1,0:T(8,128)(2,1)S(1)} %all_to_all.10.sums_ref, bf16[4,8192,128]{2,1,0:T(8,128)(2,1)S(1)} %bitcast.7, bf16[4,8192,128]{2,1,0:T(8,128)(2,1)S(1)} %bitcast.9), custom_call_target="tpu_custom_call" | custom-call | tf_op jit(solution)/shard_map/attention/pallas_call | solution.py:284
  23.7 10.3 %all_to_all.11.message_ref = bf16[16,8,1152]{2,1,0:T(8,128)(2,1)S(1)} all-to-all(bf16[16,8,1152]{2,1,0:T(8,128)(2,1)S(1)} %get-tuple-element.14), channel_id=1, replica_groups=mesh['seq'=16,'head'=8] {'seq'}, dimensions={0} | all-to-all | bytes 589824 | tf_op jit(solution)/shard_map/combine/all_to_all | solution.py:243
  34.0 0.0 copy-done
  34.1 0.5 %combine.1 = bf16[4,8,128]{2,1,0:T(8,128)(2,1)S(1)} custom-call(bf16[16,8,1152]{2,1,0:T(8,128)(2,1)S(1)} %all_to_all.11.message_ref, bf16[1024,512]{1,0:T(8,128)(2,1)S(1)} %copy-done), custom_call_target="tpu_custom_call" | custom-call | tf_op jit(solution)/shard_map/combine/pallas_call | solution.py:306
  34.5 3.3 %collective-permute-start = (bf16[4,8,128]{2,1,0:T(8,128)(2,1)S(1)}, bf16[4,8,128]{2,1,0:T(8,128)(2,1)S(1)}, u32[]{:S(2)}, u32[]{:S(2)}) collective-permute-start(bf16[4,8,128]{2,1,0:T(8,128)(2,1)S(1)} %combine.1), channel_id=1, source_target_pairs={{0,1},{1,0},{2,3},{3,2},{4,5},{5,4},{6,7},{7,6},{8,9},{9,8},{10,11... | collective-permute-start | bytes 24584 | tf_op jit(solution)/shard_map/sum_over_heads/ppermute | solution.py:314
  37.8 0.8 %collective-permute-done = bf16[4,8,128]{2,1,0:T(8,128)(2,1)S(1)} collective-permute-done((bf16[4,8,128]{2,1,0:T(8,128)(2,1)S(1)}, bf16[4,8,128]{2,1,0:T(8,128)(2,1)S(1)}, u32[]{:S(2)}, u32[]{:S(2)}) %collective-permute-start) | collective-permute-done | bytes 8224 | tf_op jit(solution)/shard_map/sum_over_heads/ppermute | solution.py:314
  38.6 3.1 %collective-permute-start.3 = (f32[8,128]{1,0:T(8,128)S(1)}, f32[8,128]{1,0:T(8,128)S(1)}, u32[]{:S(2)}, u32[]{:S(2)}) collective-permute-start(f32[8,128]{1,0:T(8,128)S(1)} %get-tuple-element.17), channel_id=1, source_target_pairs={{0,5},{1,4},{2,7},{3,6},{4,1},{5,0},{6,3},{7,2},{8,13},{9,12},{10,... | collective-permute-start | bytes 12296 | tf_op jit(solution)/shard_map/sum_over_heads/ppermute | solution.py:319
  41.8 0.8 %collective-permute-start.2 = (f32[8,128]{1,0:T(8,128)S(1)}, f32[8,128]{1,0:T(8,128)S(1)}, u32[]{:S(2)}, u32[]{:S(2)}) collective-permute-start(f32[8,128]{1,0:T(8,128)S(1)} %get-tuple-element.18), channel_id=1, source_target_pairs={{0,6},{1,7},{2,4},{3,5},{4,2},{5,3},{6,0},{7,1},{8,14},{9,15},{10,... | collective-permute-start | bytes 12296 | tf_op jit(solution)/shard_map/sum_over_heads/ppermute | solution.py:319
  42.6 0.0 collective-permute-start.1
  42.6 0.6 %collective-permute-done.3.part3_ref = f32[8,128]{1,0:T(8,128)S(1)} collective-permute-done((f32[8,128]{1,0:T(8,128)S(1)}, f32[8,128]{1,0:T(8,128)S(1)}, u32[]{:S(2)}, u32[]{:S(2)}) %collective-permute-start.3) | collective-permute-done | bytes 4128 | tf_op jit(solution)/shard_map/sum_over_heads/ppermute | solution.py:319
  43.2 2.3 %collective-permute-done.2.part2_ref = f32[8,128]{1,0:T(8,128)S(1)} collective-permute-done((f32[8,128]{1,0:T(8,128)S(1)}, f32[8,128]{1,0:T(8,128)S(1)}, u32[]{:S(2)}, u32[]{:S(2)}) %collective-permute-start.2) | collective-permute-done | bytes 4128 | tf_op jit(solution)/shard_map/sum_over_heads/ppermute | solution.py:319
  45.5 0.0 collective-permute-done.1.part1_ref
  45.5 0.7 %sum_over_heads.1 = bf16[2,4,64]{2,1,0:T(4,128)(2,1)} custom-call(f32[4,8,128]{2,1,0:T(8,128)S(1)} %convert_add_fusion.pair_ref, f32[8,128]{1,0:T(8,128)S(1)} %collective-permute-done.1.part1_ref, f32[8,128]{1,0:T(8,128)S(1)} %collective-permute-done.2.part2_ref, f32[8,128]{1,0:T(8,128)S(1)} %collective-permute-done.3.part3_ref), custom_call_target="tpu_custom_call" | custom-call | tf_op jit(solution)/shard_map/sum_over_heads/pallas_call | solution.py:320
  (7 shorter events, 0.0 us)
Async XLA Ops:
  2.4 17.0 %slice-start = ((s8[8388608]{0:T(1024)(128)(4,1)}), s8[4194304]{0:T(1024)(128)(4,1)S(1)}, s32[]{:S(2)}) async-start(s8[8388608]{0:T(1024)(128)(4,1)} %bitcast.6), calls=%async_computation.2 | async-start | bytes 8388608
  2.4 17.0 %slice-start.2 = ((s8[8388608]{0:T(1024)(128)(4,1)}), s8[4194304]{0:T(1024)(128)(4,1)S(1)}, s32[]{:S(2)}) async-start(s8[8388608]{0:T(1024)(128)(4,1)} %bitcast.8), calls=%async_computation.4 | async-start | bytes 8388608
  2.4 17.0 %slice-start.1 = ((s8[8388608]{0:T(1024)(128)(4,1)}), s8[4194304]{0:T(1024)(128)(4,1)S(1)}, s32[]{:S(2)}) async-start(s8[8388608]{0:T(1024)(128)(4,1)} %bitcast.6), calls=%async_computation.3 | async-start | bytes 8388608
  2.4 17.0 %slice-start.3 = ((s8[8388608]{0:T(1024)(128)(4,1)}), s8[4194304]{0:T(1024)(128)(4,1)S(1)}, s32[]{:S(2)}) async-start(s8[8388608]{0:T(1024)(128)(4,1)} %bitcast.8), calls=%async_computation.5 | async-start | bytes 8388608
  19.4 14.6 %copy-start = (bf16[1024,512]{1,0:T(8,128)(2,1)S(1)}, bf16[1024,512]{1,0:T(8,128)(2,1)}, u32[]{:S(2)}) copy-start(bf16[1024,512]{1,0:T(8,128)(2,1)} %w_out_ref.1) | copy-start | bytes 3145732
  34.5 4.1 %collective-permute-start = (bf16[4,8,128]{2,1,0:T(8,128)(2,1)S(1)}, bf16[4,8,128]{2,1,0:T(8,128)(2,1)S(1)}, u32[]{:S(2)}, u32[]{:S(2)}) collective-permute-start(bf16[4,8,128]{2,1,0:T(8,128)(2,1)S(1)} %combine.1), channel_id=1, source_target_pairs={{0,1},{1,0},{2,3},{3,2},{4,5},{5,4},{6,7},{7,6},{8,9},{9,8},{10,11... | collective-permute-start | bytes 24584 | tf_op jit(solution)/shard_map/sum_over_heads/ppermute | solution.py:314
  38.6 4.5 %collective-permute-start.3 = (f32[8,128]{1,0:T(8,128)S(1)}, f32[8,128]{1,0:T(8,128)S(1)}, u32[]{:S(2)}, u32[]{:S(2)}) collective-permute-start(f32[8,128]{1,0:T(8,128)S(1)} %get-tuple-element.17), channel_id=1, source_target_pairs={{0,5},{1,4},{2,7},{3,6},{4,1},{5,0},{6,3},{7,2},{8,13},{9,12},{10,... | collective-permute-start | bytes 12296 | tf_op jit(solution)/shard_map/sum_over_heads/ppermute | solution.py:319
  41.8 3.7 %collective-permute-start.2 = (f32[8,128]{1,0:T(8,128)S(1)}, f32[8,128]{1,0:T(8,128)S(1)}, u32[]{:S(2)}, u32[]{:S(2)}) collective-permute-start(f32[8,128]{1,0:T(8,128)S(1)} %get-tuple-element.18), channel_id=1, source_target_pairs={{0,6},{1,7},{2,4},{3,5},{4,2},{5,3},{6,0},{7,1},{8,14},{9,15},{10,... | collective-permute-start | bytes 12296 | tf_op jit(solution)/shard_map/sum_over_heads/ppermute | solution.py:319
  42.6 2.9 %collective-permute-start.1 = (f32[8,128]{1,0:T(8,128)S(1)}, f32[8,128]{1,0:T(8,128)S(1)}, u32[]{:S(2)}, u32[]{:S(2)}) collective-permute-start(f32[8,128]{1,0:T(8,128)S(1)} %get-tuple-element.19), channel_id=1, source_target_pairs={{0,2},{1,3},{2,0},{3,1},{4,6},{5,7},{6,4},{7,5},{8,10},{9,11},{10,... | collective-permute-start | bytes 12296 | tf_op jit(solution)/shard_map/sum_over_heads/ppermute | solution.py:319
